TPU v7x, 32 devices: a whole 2x2x4 slice. The times are simulated.
32 devices in a mesh: section: 2 (over core), group: 4 (over z), rep: 4 (over y, x).
Axes of the slice: x: 2, y: 2, z: 4, core: 2. Of those that a mesh axis runs over, the one named last changes fastest.
Arguments:
- latents: bfloat16 [32, 256, 384], P(('group', 'rep')), may hold values from -6 to 6
- cond: float32 [32, 384], P(('group', 'rep')), may hold values from -6 to 6
- cotangent: bfloat16 [32, 256, 384], P(('group', 'rep')), may hold values from -6 to 6
- live_count: int32 [16, 2], P(('group', 'rep')), may hold values from 0 to 1, as said below
- adaptive_weight: bfloat16 [2, 384, 2304], P('section', 'group'), may hold values from -0.3125 to 0.3125
- adaptive_bias: bfloat16 [2, 2304], P('section', 'group'), may hold values from 0.5 to 1.5
- query_key_value_weight: bfloat16 [2, 384, 1152], P('section', 'group'), may hold values from -0.15625 to 0.15625
- output_projection_weight: bfloat16 [2, 384, 384], P('section', 'group'), may hold values from -1.25 to 1.25
- first_dense_weight: bfloat16 [2, 384, 1536], P('section', 'group'), may hold values from -0.3125 to 0.3125
- first_dense_bias: bfloat16 [2, 1536], P('section', 'group'), may hold values from -3 to 3
- second_dense_weight: bfloat16 [2, 1536, 384], P('section', 'group'), may hold values from -0.15625 to 0.15625
Outputs:
- section_outputs: bfloat16 [2, 32, 256, 384], P('section', ('group', 'rep'))
- input_grads: float32 [2, 32, 256, 384], P('section', ('group', 'rep'))
- cond_grads: float32 [2, 32, 384], P('section', ('group', 'rep'))
- grad_ada: float32 [2, 384, 2304], P('section', 'group')
- grad_bada: float32 [2, 2304], P('section', 'group')
- grad_qkv: float32 [2, 384, 1152], P('section', 'group')
- grad_proj: float32 [2, 384, 384], P('section', 'group')
- grad_fc1: float32 [2, 384, 1536], P('section', 'group')
- grad_bfc1: float32 [2, 1536], P('section', 'group')
- grad_fc2: float32 [2, 1536, 384], P('section', 'group')
Inputs may be any that keep to these rules, and one draw needn't show every extreme that they name: live_count of a device block and micro-batch counts the real latents, which fill its first slots; the rest hold no latent. In every micro-batch one device block has 1 and another has none.
All inputs are finite; a program needn't handle non-finite values.
Results may differ from a plain program's by a relative error of at most 0.018.
Values may be sent and summed in bfloat16 or wider, within the bound.
A program may use at most 192 MiB of HBM per device.

v0:
```python
from functools import partial

import jax
import jax.numpy as jnp
from jax import lax
from jax.sharding import PartitionSpec as P

D = 384
HEADS = 6
HEAD_DIM = 64
FF = 1536
TOK = 256
MB = 2
SLOTS = 1


epsilon = 1e-06


def passed_along(value, axis, steps):
    count = lax.axis_size(axis)
    first, last = (max(0, -steps), min(count, count - steps))
    return lax.ppermute(value, axis, [(source, source + steps) for source in range(first, last)])


def for_sending(x):
    return jax.tree.map(lambda a: a.astype(jnp.bfloat16) if a.dtype == jnp.float32 else a, x)


def normalize(values):
    center = values - jnp.mean(values, axis=-1, keepdims=True)
    spread = jnp.mean(center * center, axis=-1, keepdims=True)
    return center * lax.rsqrt(spread + epsilon)


def modulate(values, scale_part, shift_part):
    return normalize(values) * (1.0 + scale_part[:, None, :]) + shift_part[:, None, :]


def heads_of(array, offset):
    count, length = (array.shape[0], array.shape[1])
    return array[..., offset * D : (offset + 1) * D].reshape(count, length, HEADS, HEAD_DIM)


def attention_scores(queries, keys_part):
    scores = jnp.einsum("snhe,smhe->shnm", queries, keys_part, preferred_element_type=jnp.float32)
    return scores * HEAD_DIM ** (-0.5)


def forward_block(input_rows, condition_vector, weights):
    (
        adaptive_weight,
        adaptive_bias,
        query_key_value_weight,
        output_projection_weight,
        first_dense_weight,
        first_dense_bias,
        second_dense_weight,
    ) = weights
    silu_low = jax.nn.silu(condition_vector).astype(jnp.bfloat16)
    modulation = jnp.dot(
        silu_low, adaptive_weight, preferred_element_type=jnp.float32
    ) + adaptive_bias.astype(jnp.float32)
    shift_attn, scale_attn, gate_attn, shift_mlp, scale_mlp, gate_mlp = jnp.split(
        modulation, 6, axis=-1
    )
    widened = input_rows.astype(jnp.float32)
    normed_reduced = modulate(widened, scale_attn, shift_attn).astype(jnp.bfloat16)
    triple_low = jnp.dot(
        normed_reduced, query_key_value_weight, preferred_element_type=jnp.float32
    ).astype(jnp.bfloat16)
    queries = heads_of(triple_low, 0)
    keys_part = heads_of(triple_low, 1)
    values_part = heads_of(triple_low, 2)
    scores = attention_scores(queries, keys_part)
    highest = jnp.max(scores, axis=-1, keepdims=True)
    log_total = highest + jnp.log(jnp.sum(jnp.exp(scores - highest), axis=-1, keepdims=True))
    probs_low = jnp.exp(scores - log_total).astype(jnp.bfloat16)
    mixed = jnp.einsum(
        "shnm,smhe->snhe", probs_low, values_part, preferred_element_type=jnp.float32
    )
    mixed_reduced = mixed.reshape(input_rows.shape).astype(jnp.bfloat16)
    attended = jnp.dot(mixed_reduced, output_projection_weight, preferred_element_type=jnp.float32)
    middle = widened + gate_attn[:, None, :] * attended
    second_low = modulate(middle, scale_mlp, shift_mlp).astype(jnp.bfloat16)
    hidden = jnp.dot(
        second_low, first_dense_weight, preferred_element_type=jnp.float32
    ) + first_dense_bias.astype(jnp.float32)
    active_low = jax.nn.gelu(hidden, approximate=True).astype(jnp.bfloat16)
    branch = jnp.dot(active_low, second_dense_weight, preferred_element_type=jnp.float32)
    result = middle + gate_mlp[:, None, :] * branch
    kept_state = (
        input_rows,
        condition_vector,
        modulation,
        normed_reduced,
        triple_low,
        log_total[..., 0],
        mixed_reduced,
        attended,
        middle,
        second_low,
        hidden,
        active_low,
        branch,
    )
    return (result, kept_state)


def forward_empty(input_rows, condition_vector, weights):
    count, length = (input_rows.shape[0], input_rows.shape[1])
    rows_float = jnp.zeros((count, length, D), jnp.float32)
    rows_low = jnp.zeros((count, length, D), jnp.bfloat16)
    kept_state = (
        rows_low,
        jnp.zeros((count, D), jnp.float32),
        jnp.zeros((count, 6 * D), jnp.float32),
        rows_low,
        jnp.zeros((count, length, 3 * D), jnp.bfloat16),
        jnp.zeros((count, HEADS, length), jnp.float32),
        rows_low,
        rows_float,
        rows_float,
        rows_low,
        jnp.zeros((count, length, FF), jnp.float32),
        jnp.zeros((count, length, FF), jnp.bfloat16),
        rows_float,
    )
    return (rows_float, kept_state)


def backward_block(out_grad, kept_state, weights):
    (
        adaptive_weight,
        adaptive_bias,
        query_key_value_weight,
        output_projection_weight,
        first_dense_weight,
        first_dense_bias,
        second_dense_weight,
    ) = weights
    (
        input_rows,
        condition_vector,
        modulation,
        normed_reduced,
        triple_low,
        log_total,
        mixed_reduced,
        attended,
        middle,
        second_low,
        hidden,
        active_low,
        branch,
    ) = kept_state
    count, length = (input_rows.shape[0], input_rows.shape[1])
    shift_attn, scale_attn, gate_attn, shift_mlp, scale_mlp, gate_mlp = jnp.split(
        modulation, 6, axis=-1
    )
    grad_gate_mlp = jnp.sum(out_grad * branch, axis=1)
    branch_low = (gate_mlp[:, None, :] * out_grad).astype(jnp.bfloat16)
    grad_fc2 = jnp.einsum("snf,snd->fd", active_low, branch_low, preferred_element_type=jnp.float32)
    grad_active = jnp.einsum(
        "snd,fd->snf", branch_low, second_dense_weight, preferred_element_type=jnp.float32
    )
    unused, gelu_back = jax.vjp(partial(jax.nn.gelu, approximate=True), hidden)
    hidden_low = gelu_back(grad_active)[0].astype(jnp.bfloat16)
    grad_bias = jnp.sum(hidden_low, axis=(0, 1), dtype=jnp.float32)
    grad_fc1 = jnp.einsum("snd,snf->df", second_low, hidden_low, preferred_element_type=jnp.float32)
    grad_second = jnp.einsum(
        "snf,df->snd", hidden_low, first_dense_weight, preferred_element_type=jnp.float32
    )
    unused, norm_back = jax.vjp(modulate, middle, scale_mlp, shift_mlp)
    grad_middle, grad_scale_mlp, grad_shift_mlp = norm_back(grad_second)
    grad_middle = grad_middle + out_grad
    grad_gate_attn = jnp.sum(grad_middle * attended, axis=1)
    attended_reduced = (gate_attn[:, None, :] * grad_middle).astype(jnp.bfloat16)
    grad_proj = jnp.einsum(
        "row,rol->wl", mixed_reduced, attended_reduced, preferred_element_type=jnp.float32
    )
    mixed_grad_low = jnp.einsum(
        "lqa,ia->lqi",
        attended_reduced,
        output_projection_weight,
        preferred_element_type=jnp.float32,
    ).astype(jnp.bfloat16)
    heads_grad = mixed_grad_low.reshape(count, length, HEADS, HEAD_DIM)
    queries = heads_of(triple_low, 0)
    keys_part = heads_of(triple_low, 1)
    values_part = heads_of(triple_low, 2)
    probs = jnp.exp(attention_scores(queries, keys_part) - log_total[..., None])
    probs_low = probs.astype(jnp.bfloat16)
    grad_values = jnp.einsum(
        "shnm,snhe->smhe", probs_low, heads_grad, preferred_element_type=jnp.float32
    )
    grad_probs = jnp.einsum(
        "snhe,smhe->shnm", heads_grad, values_part, preferred_element_type=jnp.float32
    )
    scores_low = (
        probs * (grad_probs - jnp.sum(grad_probs * probs, axis=-1, keepdims=True))
    ).astype(jnp.bfloat16)
    grad_queries = jnp.einsum(
        "shnm,smhe->snhe", scores_low, keys_part, preferred_element_type=jnp.float32
    ) * HEAD_DIM ** (-0.5)
    grad_keys = jnp.einsum(
        "shnm,snhe->smhe", scores_low, queries, preferred_element_type=jnp.float32
    ) * HEAD_DIM ** (-0.5)
    triple_gradient_reduced = jnp.concatenate(
        [
            grad_queries.reshape(count, length, D),
            grad_keys.reshape(count, length, D),
            grad_values.reshape(count, length, D),
        ],
        axis=-1,
    ).astype(jnp.bfloat16)
    grad_qkv = jnp.einsum(
        "row,rol->wl", normed_reduced, triple_gradient_reduced, preferred_element_type=jnp.float32
    )
    grad_normed = jnp.einsum(
        "lqa,ia->lqi",
        triple_gradient_reduced,
        query_key_value_weight,
        preferred_element_type=jnp.float32,
    )
    unused, first_back = jax.vjp(modulate, input_rows.astype(jnp.float32), scale_attn, shift_attn)
    grad_inputs, grad_scale_attn, grad_shift_attn = first_back(grad_normed)
    grad_inputs = grad_inputs + grad_middle
    modulation_low = jnp.concatenate(
        [
            grad_shift_attn,
            grad_scale_attn,
            grad_gate_attn,
            grad_shift_mlp,
            grad_scale_mlp,
            grad_gate_mlp,
        ],
        axis=-1,
    ).astype(jnp.bfloat16)
    grad_bada = jnp.sum(modulation_low, axis=0, dtype=jnp.float32)
    silu_low = jax.nn.silu(condition_vector).astype(jnp.bfloat16)
    grad_ada = jnp.dot(silu_low.T, modulation_low, preferred_element_type=jnp.float32)
    grad_silu = jnp.dot(modulation_low, adaptive_weight.T, preferred_element_type=jnp.float32)
    unused, silu_back = jax.vjp(jax.nn.silu, condition_vector)
    grad_condition = silu_back(grad_silu)[0]
    return (
        grad_inputs,
        grad_condition,
        (grad_ada, grad_bada, grad_qkv, grad_proj, grad_fc1, grad_bias, grad_fc2),
    )


def backward_empty(out_grad, kept_state, weights):
    count = out_grad.shape[0]
    grads = tuple((jnp.zeros(array.shape, jnp.float32) for array in weights))
    return (jnp.zeros(out_grad.shape, jnp.float32), jnp.zeros((count, D), jnp.float32), grads)


def stripped(gathered):
    return tuple((array[0] for array in gathered))


def body(
    latents,
    cond,
    cotangent,
    live_count,
    adaptive_weight,
    adaptive_bias,
    query_key_value_weight,
    output_projection_weight,
    first_dense_weight,
    first_dense_bias,
    second_dense_weight,
):
    is_first = lax.axis_index("section") == 0
    inputs_all = latents.reshape(MB, SLOTS, TOK, D)
    conds_all = cond.reshape(MB, SLOTS, D)
    tangents_all = cotangent.reshape(MB, SLOTS, TOK, D)
    live = (jnp.arange(SLOTS, dtype=jnp.int32)[None, :] < live_count[0][:, None]).astype(
        jnp.float32
    )
    kept_weights = stripped(
        (
            lax.all_gather(adaptive_weight, "group", axis=1, tiled=True),
            lax.all_gather(adaptive_bias, "group", axis=1, tiled=True),
            lax.all_gather(query_key_value_weight, "group", axis=1, tiled=True),
            lax.all_gather(output_projection_weight, "group", axis=1, tiled=True),
            lax.all_gather(first_dense_weight, "group", axis=1, tiled=True),
            lax.all_gather(first_dense_bias, "group", axis=1, tiled=True),
            lax.all_gather(second_dense_weight, "group", axis=1, tiled=True),
        )
    )
    received = jnp.zeros((SLOTS, TOK, D), jnp.bfloat16)
    forward_out = []
    states = []
    for moment in range(MB + 1):
        weights = kept_weights
        own_rows = inputs_all[min(moment, MB - 1)]
        rows_in = jnp.where(is_first, own_rows, received)
        cond_in = jnp.where(is_first, conds_all[min(moment, MB - 1)], conds_all[max(moment - 1, 0)])
        active = jnp.where(is_first, moment < MB, moment >= 1)
        result, kept_state = lax.cond(
            active, forward_block, forward_empty, rows_in, cond_in, weights
        )
        result_low = result.astype(jnp.bfloat16)
        forward_out.append(result_low)
        states.append(kept_state)
        if moment < MB:
            received = passed_along(result_low, "section", 1)
    grad_recv = jnp.zeros((SLOTS, TOK, D), jnp.bfloat16)
    cond_recv = jnp.zeros((SLOTS, D), jnp.bfloat16)
    backward_out = []
    owned = None
    totals = None
    for moment in range(MB + 1):
        weights = kept_weights
        earlier = max(MB - 1 - moment, 0)
        out_grad = jnp.where(
            is_first,
            grad_recv.astype(jnp.float32),
            tangents_all[earlier].astype(jnp.float32) * live[earlier][:, None, None],
        )
        kept_state = states[MB - moment]
        active = jnp.where(is_first, moment >= 1, moment < MB)
        grad_rows, grad_cond, grads = lax.cond(
            active, backward_block, backward_empty, out_grad, kept_state, weights
        )
        rows_low = grad_rows.astype(jnp.bfloat16)
        cond_low = grad_cond.astype(jnp.bfloat16)
        backward_out.append((grad_rows, grad_cond, rows_low, cond_low, cond_recv))
        totals = (
            grads
            if totals is None
            else jax.tree.map(lambda former, latter: former + latter, totals, grads)
        )
        if moment < MB:
            grad_recv, cond_recv = passed_along((rows_low, cond_low), "section", -1)
    owned = jax.tree.map(
        lambda part: part.astype(jnp.float32),
        lax.psum_scatter(for_sending(totals), "group", scatter_dimension=0, tiled=True),
    )
    owned = jax.tree.map(lambda part: part.astype(jnp.float32), lax.psum(for_sending(owned), "rep"))
    outputs_list = []
    input_list = []
    cond_list = []
    for batch in range(MB):
        alive = live[batch].astype(jnp.bfloat16)[:, None, None]
        outputs_list.append(jnp.where(is_first, forward_out[batch], forward_out[batch + 1]) * alive)
        early = backward_out[MB - batch]
        late = backward_out[MB - 1 - batch]
        input_list.append(jnp.where(is_first, early[0], late[2].astype(jnp.float32)))
        cond_list.append(
            jnp.where(
                is_first, early[1] + early[4].astype(jnp.float32), late[3].astype(jnp.float32)
            )
        )
    section_outputs = jnp.concatenate(outputs_list, axis=0)[None]
    input_grads = jnp.concatenate(input_list, axis=0)[None]
    cond_grads = jnp.concatenate(cond_list, axis=0)[None]
    return (
        section_outputs,
        input_grads,
        cond_grads,
        owned[0][None],
        owned[1][None],
        owned[2][None],
        owned[3][None],
        owned[4][None],
        owned[5][None],
        owned[6][None],
    )


def solution(mesh):
    return jax.shard_map(
        body,
        mesh=mesh,
        in_specs=(
            P(("group", "rep"), None, None),
            P(("group", "rep"), None),
            P(("group", "rep"), None, None),
            P(("group", "rep"), None),
            P("section", "group", None),
            P("section", "group"),
            P("section", "group", None),
            P("section", "group", None),
            P("section", "group", None),
            P("section", "group"),
            P("section", "group", None),
        ),
        out_specs=(
            P("section", ("group", "rep"), None, None),
            P("section", ("group", "rep"), None, None),
            P("section", ("group", "rep"), None),
            P("section", "group", None),
            P("section", "group"),
            P("section", "group", None),
            P("section", "group", None),
            P("section", "group", None),
            P("section", "group"),
            P("section", "group", None),
        ),
        check_vma=False,
    )
```

profile of v0, /device:TPU:0, one launch (start us, length us, event | category | flops | bytes accessed | tf_op | source)
XLA Modules:
  0.0 574.1 jit_solution(1712281635695127555)
XLA Ops:
  12.1 13.8 %all_gather.26 = bf16[1,1536]{1,0:T(2,128)(2,1)S(1)} all-gather(bf16[1,384]{1,0:T(2,128)(2,1)} %param.28), channel_id=1, replica_groups=mesh['section'=2,'group'=4,'rep'=4] {'group'}, dimensions={1}, use_global_device_ids=true | all-gather | bytes 3840 | tf_op jit(solution)/shard_map/all_gather | solution.py:290
  30.5 11.2 %all-reduce = bf16[2304]{0:T(1024)(128)(2,1)S(1)} all-reduce(bf16[2304]{0:T(1024)(128)(2,1)S(1)} %dynamic-update-slice), channel_id=1, replica_groups=mesh['section'=2,'group'=4,'rep'=4] {'group'}, use_global_device_ids=true, to_apply=%add | all-reduce | flops 2304 | bytes 9216 | tf_op jit(solution)/shard_map/squeeze | solution.py:260
  41.6 14.0 %all_gather.24 = bf16[1,384,384]{2,1,0:T(8,128)(2,1)S(1)} all-gather(bf16[1,96,384]{2,1,0:T(8,128)(2,1)S(1)} %copy-done.114), channel_id=1, replica_groups=mesh['section'=2,'group'=4,'rep'=4] {'group'}, dimensions={1}, use_global_device_ids=true | all-gather | bytes 368640 | tf_op jit(solution)/shard_map/all_gather | solution.py:288
  57.5 31.4 %all_gather.23 = bf16[1,384,1152]{2,1,0:T(8,128)(2,1)S(1)} all-gather(bf16[1,96,1152]{2,1,0:T(8,128)(2,1)S(1)} %copy-done.102), channel_id=1, replica_groups=mesh['section'=2,'group'=4,'rep'=4] {'group'}, dimensions={1}, use_global_device_ids=true | all-gather | bytes 1105920 | tf_op jit(solution)/shard_map/all_gather | solution.py:287
  88.9 41.7 %all-gather.4.cloned.1.call-done = bf16[1,384,2304]{2,1,0:T(8,128)(2,1)} async-done(((bf16[1,96,2304]{2,1,0:T(8,128)(2,1)}), bf16[1,384,2304]{2,1,0:T(8,128)(2,1)}) %all-gather.4.cloned.1.call-update) | async-done | bytes 1769488 | tf_op jit(solution)/shard_map/all_gather | solution.py:285
  130.6 13.2 %conditional.4 = (bf16[1,256,384]{2,1,0:T(8,128)(2,1)S(1)}, f32[1,384]{1,0:T(1,128)}, f32[1,2304]{1,0:T(1,128)S(1)}, bf16[1,256,384]{2,1,0:T(8,128)(2,1)}, bf16[...) conditional(s32[]{:T(128)} %convert_element_type.491, () %tuple.65, ...), branch_computations={%region_0.1_spmd, %region_1.8_spmd} | conditional | flops 1021386368 | bytes 41346496 | solution.py:303
  138.9 2.8 fusion.16
  157.7 10.5 %conditional.5 = (bf16[1,256,384]{2,1,0:T(8,128)(2,1)S(1)}, f32[1,384]{1,0:T(1,128)}, f32[1,2304]{1,0:T(1,128)}, bf16[1,256,384]{2,1,0:T(8,128)(2,1)}, bf16[1,25...) conditional(s32[]{:T(128)} %convert_element_type.509, () %tuple.67, ...), branch_computations={%region_14.15_spmd, %region_15.22_spmd} | conditional | flops 1021386368 | bytes 41874824 | solution.py:303
  168.2 9.5 %conditional.6 = (f32[384,2304]{1,0:T(8,128)}, f32[2304]{0:T(1024)S(1)}, f32[1536]{0:T(1024)S(1)}, bf16[1,256,384]{2,1,0:T(8,128)(2,1)S(1)}, bf16[1,384]{1,0:T(2...) conditional(s32[]{:T(128)} %convert_element_type.509, () %tuple.70, ...), branch_computations={%region_22.23_spmd, %region_23.40_spmd} | conditional | flops 2089162752 | bytes 87958680 | solution.py:326
  179.1 92.9 %collective-permute-done.2 = bf16[1,256,384]{2,1,0:T(8,128)(2,1)S(1)} collective-permute-done((bf16[1,256,384]{2,1,0:T(8,128)(2,1)S(1)}, bf16[1,256,384]{2,1,0:T(8,128)(2,1)S(1)}, u32[]{:S(2)}, u32[]{:S(2)}) %collective-permute-start.2) | collective-permute-done | bytes 196640 | tf_op jit(solution)/shard_map/ppermute | solution.py:23
  272.1 4.6 convert_reduce_fusion.8
  278.7 2.1 fusion.169
  294.9 58.1 %conditional.7 = (f32[1,256,384]{2,1,0:T(8,128)}, f32[1,384]{1,0:T(1,128)}, f32[384,2304]{1,0:T(8,128)}, f32[2304]{0:T(1024)}, f32[1536]{0:T(1024)}, /*index=5*/...) conditional(s32[]{:T(128)} %convert_element_type.491, () %tuple.69, ...), branch_computations={%region_45.46_spmd, %region_46.63_spmd} | conditional | flops 2088473856 | bytes 92844544 | solution.py:326
  302.2 3.6 convert_reduce_fusion.5
  319.5 2.1 copy.164
  321.6 2.1 copy.131
  338.5 3.3 convolution_bitcast_fusion.5
  341.8 3.2 copy.168
  347.0 3.2 copy.166
  350.2 2.9 broadcast_multiply_fusion.7
  353.0 2.3 add_convert_fusion.7
  355.5 3.7 add_convert_fusion.6
  359.7 4.1 add_convert_fusion.5
  363.9 5.6 add_convert_fusion.4
  371.9 4.9 add_convert_fusion.3
  381.3 18.7 %reduce-scatter.8.cloned.1.call-done = bf16[96,1152]{1,0:T(8,128)(2,1)} async-done(((bf16[384,1152]{1,0:T(8,128)(2,1)}), bf16[96,1152]{1,0:T(8,128)(2,1)}) %reduce-scatter.8.cloned.1.call-update) | async-done | bytes 221200 | tf_op jit(solution)/shard_map/reduce_scatter | solution.py:341
  399.9 30.4 %reduce-scatter.12.cloned.1.call-done = bf16[96,1536]{1,0:T(8,128)(2,1)} async-done(((bf16[384,1536]{1,0:T(8,128)(2,1)}), bf16[96,1536]{1,0:T(8,128)(2,1)}) %reduce-scatter.12.cloned.1.call-update) | async-done | bytes 294928 | tf_op jit(solution)/shard_map/reduce_scatter | solution.py:341
  430.3 30.3 %reduce-scatter.14.cloned.1.call-done = bf16[384,384]{1,0:T(8,128)(2,1)} async-done(((bf16[1536,384]{1,0:T(8,128)(2,1)}), bf16[384,384]{1,0:T(8,128)(2,1)}) %reduce-scatter.14.cloned.1.call-update) | async-done | bytes 294928 | tf_op jit(solution)/shard_map/reduce_scatter | solution.py:341
  460.6 39.5 %reduce-scatter.6.cloned.1.call-done = bf16[96,2304]{1,0:T(8,128)(2,1)} async-done(((bf16[384,2304]{1,0:T(8,128)(2,1)}), bf16[96,2304]{1,0:T(8,128)(2,1)}) %reduce-scatter.6.cloned.1.call-update) | async-done | bytes 442384 | tf_op jit(solution)/shard_map/reduce_scatter | solution.py:341
  503.4 17.0 %all-reduce.5 = (bf16[2304]{0:T(1024)(128)(2,1)S(1)}, bf16[1536]{0:T(1024)(128)(2,1)S(1)}) all-reduce(bf16[2304]{0:T(1024)(128)(2,1)S(1)} %add_convert_fusion.9, bf16[1536]{0:T(1024)(128)(2,1)S(1)} %add_convert_fusion.10), channel_id=3, replica_groups=mesh['section'=2,'group'=4,'rep'=4] {'group'}, use_global_device_ids=true, to_apply=%region_71.72.clone | all-reduce | flops 3840 | bytes 15360
  520.6 9.8 %all-reduce.3 = (bf16[1,576]{1,0:T(2,128)(2,1)S(1)}, bf16[1,384]{1,0:T(2,128)(2,1)S(1)}) all-reduce(bf16[1,576]{1,0:T(2,128)(2,1)S(1)} %broadcast_in_dim.142, bf16[1,384]{1,0:T(2,128)(2,1)S(1)} %broadcast_in_dim.172), channel_id=1, replica_groups=mesh['section'=2,'group'=4,'rep'=4] {'rep'}, use_global_device_ids=true, to_apply=%region_72.73 | all-reduce | flops 960 | bytes 3840 | tf_op jit(solution)/shard_map/psum | solution.py:343
  534.8 26.3 %all-reduce.8.cloned.1.call-done = (bf16[1,96,2304]{2,1,0:T(8,128)(2,1)}, bf16[1,96,1152]{2,1,0:T(8,128)(2,1)}, bf16[1,96,384]{2,1,0:T(8,128)(2,1)}, bf16[1,96,1536]{2,1,0:T(8,128)(2,1)}, bf16[1,384,384]{2,1,0:T(8,128)(2,1)}) async-done(((bf16[1,96,2304]{2,1,0:T(8,128)(2,1)}, bf16[1,96,1152]{2,1,0:T(8,128)(2,1)}, bf16[1,96,384]{2,1,0:T(8,128)(2,1)}, bf16[1,96,1536]{2,1,0:T(8,128)(2,1)}, ...) | async-done | bytes 1327120 | tf_op jit(solution)/shard_map/psum | solution.py:343
  (517 shorter events, 126.7 us)
Async XLA Ops:
  7.2 123.4 %copy-start.64 = (bf16[2,256,384]{2,1,0:T(8,128)(2,1)S(1)}, bf16[2,256,384]{2,1,0:T(8,128)(2,1)}, u32[]{:S(2)}) copy-start(bf16[2,256,384]{2,1,0:T(8,128)(2,1)} %param.19) | copy-start | bytes 1179652
  7.2 34.4 %copy-start.114 = (bf16[1,96,384]{2,1,0:T(8,128)(2,1)S(1)}, bf16[1,96,384]{2,1,0:T(8,128)(2,1)}, u32[]{:S(2)}) copy-start(bf16[1,96,384]{2,1,0:T(8,128)(2,1)} %param.26) | copy-start | bytes 221188
  7.2 48.5 %copy-start.150 = (f32[2,384]{1,0:T(2,128)S(1)}, f32[2,384]{1,0:T(2,128)}, u32[]{:S(2)}) copy-start(f32[2,384]{1,0:T(2,128)} %param.20) | copy-start | bytes 9220
  7.2 50.3 %copy-start.102 = (bf16[1,96,1152]{2,1,0:T(8,128)(2,1)S(1)}, bf16[1,96,1152]{2,1,0:T(8,128)(2,1)}, u32[]{:S(2)}) copy-start(bf16[1,96,1152]{2,1,0:T(8,128)(2,1)} %param.25) | copy-start | bytes 663556
  7.2 81.6 %all-gather.6.cloned.1.call-start = ((), (), s32[]{:S(2)}) async-start(), calls=%async_computation.6 | async-start | bytes 1474560 | tf_op jit(solution)/shard_map/all_gather | solution.py:289
  8.0 80.9 %all-gather.8.cloned.1.call-start = ((), (), s32[]{:S(2)}) async-start(), calls=%async_computation.7 | async-start | bytes 1474560 | tf_op jit(solution)/shard_map/all_gather | solution.py:291
  8.7 121.8 %all-gather.4.cloned.1.call-start = ((), (), s32[]{:S(2)}) async-start(), calls=%async_computation.5 | async-start | bytes 2211840 | tf_op jit(solution)/shard_map/all_gather | solution.py:285
  9.4 371.8 %reduce-scatter.10.cloned.1.call-start = ((), (), s32[]{:S(2)}) async-start(), calls=%async_computation.10 | async-start | bytes 368640 | tf_op jit(solution)/shard_map/reduce_scatter | solution.py:341
  25.9 104.6 %copy-start.115 = (bf16[1536]{0:T(1024)(128)(2,1)}, bf16[1536]{0:T(1024)(128)(2,1)S(1)}, u32[]{:S(2)}) copy-start(bf16[1536]{0:T(1024)(128)(2,1)S(1)} %reduce.132) | copy-start | bytes 9220
  55.7 95.3 %copy-start.1 = (bf16[1,384,384]{2,1,0:T(8,128)(2,1)}, bf16[1,384,384]{2,1,0:T(8,128)(2,1)S(1)}, u32[]{:S(2)}) copy-start(bf16[1,384,384]{2,1,0:T(8,128)(2,1)S(1)} %all_gather.24) | copy-start | bytes 884740
  88.9 59.8 %copy-start.6 = (bf16[1,384,1152]{2,1,0:T(8,128)(2,1)}, bf16[1,384,1152]{2,1,0:T(8,128)(2,1)S(1)}, u32[]{:S(2)}) copy-start(bf16[1,384,1152]{2,1,0:T(8,128)(2,1)S(1)} %all_gather.23) | copy-start | bytes 2654212
  144.3 3.9 collective-permute-start
  155.3 2.3 collective-permute-start.1
  177.7 94.3 %copy-start.110 = (f32[2304]{0:T(1024)}, f32[2304]{0:T(1024)S(1)}, u32[]{:S(2)}) copy-start(f32[2304]{0:T(1024)S(1)} %get-tuple-element.381) | copy-start | bytes 27652
  177.7 94.3 %copy-start.127 = (f32[1536]{0:T(1024)}, f32[1536]{0:T(1024)S(1)}, u32[]{:S(2)}) copy-start(f32[1536]{0:T(1024)S(1)} %get-tuple-element.389) | copy-start | bytes 18436
  177.7 94.3 %collective-permute-start.2 = (bf16[1,256,384]{2,1,0:T(8,128)(2,1)S(1)}, bf16[1,256,384]{2,1,0:T(8,128)(2,1)S(1)}, u32[]{:S(2)}, u32[]{:S(2)}) collective-permute-start(bf16[1,256,384]{2,1,0:T(8,128)(2,1)S(1)} %get-tuple-element.363), channel_id=1, source_target_pairs={{16,0},{17,1},{18,2},{19,3},{20,4},{21,5},{22,6},{23,7},{24,8},{25... | collective-permute-start | bytes 589832 | tf_op jit(solution)/shard_map/ppermute | solution.py:23
  272.0 6.7 %copy-start.91 = (bf16[1,256,384]{2,1,0:T(8,128)(2,1)}, bf16[1,256,384]{2,1,0:T(8,128)(2,1)S(1)}, u32[]{:S(2)}) copy-start(bf16[1,256,384]{2,1,0:T(8,128)(2,1)S(1)} %collective-permute-done.2) | copy-start | bytes 589828
  290.7 3.3 collective-permute-start.3
  328.5 5.8 %copy-start.172 = (f32[1,384]{1,0:T(1,128)S(1)}, f32[1,384]{1,0:T(1,128)}, u32[]{:S(2)}) copy-start(f32[1,384]{1,0:T(1,128)} %get-tuple-element.680) | copy-start | bytes 4612 | tf_op jit(solution)/shard_map/cond
  355.4 44.5 %reduce-scatter.8.cloned.1.call-start = ((), (), s32[]{:S(2)}) async-start(), calls=%async_computation.9 | async-start | bytes 1105920 | tf_op jit(solution)/shard_map/reduce_scatter | solution.py:341
  359.3 71.1 %reduce-scatter.12.cloned.1.call-start = ((), (), s32[]{:S(2)}) async-start(), calls=%async_computation.11 | async-start | bytes 1474560 | tf_op jit(solution)/shard_map/reduce_scatter | solution.py:341
  363.8 96.8 %reduce-scatter.14.cloned.1.call-start = ((), (), s32[]{:S(2)}) async-start(), calls=%async_computation.12 | async-start | bytes 1474560 | tf_op jit(solution)/shard_map/reduce_scatter | solution.py:341
  369.6 130.5 %reduce-scatter.6.cloned.1.call-start = ((), (), s32[]{:S(2)}) async-start(), calls=%async_computation.8 | async-start | bytes 2211840 | tf_op jit(solution)/shard_map/reduce_scatter | solution.py:341
  376.9 123.2 %copy-start.149 = (f32[1,384]{1,0:T(1,128)S(1)}, f32[1,384]{1,0:T(1,128)}, u32[]{:S(2)}) copy-start(f32[1,384]{1,0:T(1,128)} %get-tuple-element.688) | copy-start | bytes 4612
  376.9 184.3 %all-reduce.8.cloned.1.call-start = ((), (), s32[]{:S(2)}) async-start(), calls=%async_computation.13 | async-start | bytes 2654208 | tf_op jit(solution)/shard_map/psum | solution.py:343
  379.0 152.5 %collective-permute-start.5 = (bf16[1,384]{1,0:T(2,128)(2,1)S(1)}, bf16[1,384]{1,0:T(2,128)(2,1)S(1)}, u32[]{:S(2)}, u32[]{:S(2)}) collective-permute-start(bf16[1,384]{1,0:T(2,128)(2,1)S(1)} %copy-done.183), channel_id=1, source_target_pairs={{16,0},{17,1},{18,2},{19,3},{20,4},{21,5},{22,6},{23,7},{24,8},{25... | collective-permute-start | bytes 2312 | tf_op jit(solution)/shard_map/ppermute | solution.py:23
  381.2 120.8 %copy-start.128 = (f32[1536]{0:T(1024)S(1)}, f32[1536]{0:T(1024)}, u32[]{:S(2)}) copy-start(f32[1536]{0:T(1024)} %copy-done.127) | copy-start | bytes 18436
  381.2 120.8 %copy-start.171 = (f32[1536]{0:T(1024)S(1)}, f32[1536]{0:T(1024)}, u32[]{:S(2)}) copy-start(f32[1536]{0:T(1024)} %get-tuple-element.772) | copy-start | bytes 18436
  500.1 31.5 %copy-start.173 = (f32[1,384]{1,0:T(1,128)S(1)}, f32[1,384]{1,0:T(1,128)}, u32[]{:S(2)}) copy-start(f32[1,384]{1,0:T(1,128)} %get-tuple-element.378) | copy-start | bytes 4612
  500.1 32.8 %copy-start.76 = (bf16[1,256,384]{2,1,0:T(8,128)(2,1)S(1)}, bf16[1,256,384]{2,1,0:T(8,128)(2,1)}, u32[]{:S(2)}) copy-start(bf16[1,256,384]{2,1,0:T(8,128)(2,1)} %copy-done.75) | copy-start | bytes 589828
  500.1 33.8 %copy-start.55 = (f32[1,256,384]{2,1,0:T(8,128)S(1)}, f32[1,256,384]{2,1,0:T(8,128)}, u32[]{:S(2)}) copy-start(f32[1,256,384]{2,1,0:T(8,128)} %get-tuple-element.748) | copy-start | bytes 1179652
  500.7 30.9 %collective-permute-start.4 = (bf16[1,384]{1,0:T(2,128)(2,1)S(1)}, bf16[1,384]{1,0:T(2,128)(2,1)S(1)}, u32[]{:S(2)}, u32[]{:S(2)}) collective-permute-start(bf16[1,384]{1,0:T(2,128)(2,1)S(1)} %get-tuple-element.770), channel_id=1, source_target_pairs={{16,0},{17,1},{18,2},{19,3},{20,4},{21,5},{22,6},{23,7},{24,8},{25... | collective-permute-start | bytes 2312 | tf_op jit(solution)/shard_map/ppermute | solution.py:23
  (137 other events, 370.2 us)
Sparse Core Ops, SparseCore 0:
  9.6 34.4 all-gather.5
  45.7 42.9 all-gather.7
  90.3 40.1 all-gather.3
  355.5 18.7 reduce-scatter.9
  377.0 22.8 reduce-scatter.7
  402.1 28.2 reduce-scatter.11
  432.7 27.9 reduce-scatter.13
  462.9 37.0 reduce-scatter.5
  504.1 57.0 all-reduce.7
where the time goes:
time: 584 us; the launch traced here: 574 us
  waiting for transfers between devices  284 us (49%)
  blocking collectives  97.2 us (17%)
  matrix products  60.4 us (10%)
  local copies, waits for them, and re-layouts  52.3 us (9%)
  other arithmetic  51.3 us (9%)
  between operations  18.8 us (3%)
  starting transfers between devices  8.67 us (1%)
    reduce_scatter x5, waiting for transfers between devices, body(): lax.psum_scatter(for_sending(totals), 'group', scatter_dimension=0, tiled...  119 us
    ppermute x6, waiting for transfers between devices, passed_along(): lax.ppermute(value, axis, [(source, source + steps) for source in range(f...  95.2 us
    all_gather x1, waiting for transfers between devices, body(): lax.all_gather(adaptive_weight, 'group', axis=1, tiled=True)  41.7 us
    all_gather x1, blocking collectives, body(): lax.all_gather(query_key_value_weight, 'group', axis=1, tiled=True)  31.4 us
    psum x1, waiting for transfers between devices, body(): lax.psum(for_sending(owned), 'rep')  26.3 us
    another operation x26, local copies, waits for them, and re-layouts  21.6 us
    unnamed x1, blocking collectives  17 us
    all_gather x1, blocking collectives, body(): lax.all_gather(output_projection_weight, 'group', axis=1, tiled=True)  14 us
  transfers between devices with their start and end apart: 15, of which 9 were waited for; matrix products, arithmetic and copies ran while one was open for 7% of the time, Pallas kernels for 0%

commit v1 on v0

v1 whole, which is shorter than its diff:
```python
from functools import partial

import jax
import jax.numpy as jnp
from jax import lax
from jax.experimental import pallas as pl
from jax.experimental.pallas import tpu as pltpu
from jax.sharding import PartitionSpec as P

D = 384
HEADS = 6
HEAD_DIM = 64
FF = 1536
TOK = 256
EPS = 1e-06
F32 = jnp.float32
BF16 = jnp.bfloat16
NN = (((1,), (0,)), ((), ()))
NT = (((1,), (1,)), ((), ()))
TN = (((0,), (0,)), ((), ()))
GELU_A = 0.7978845608028654
GELU_B = 0.044715


def dot(a, b, dims=NN):
    return lax.dot_general(a, b, dims, preferred_element_type=F32)


def cols(j, width=D):
    return slice(j * width, (j + 1) * width)


def layer_norm(x):
    center = x - jnp.mean(x, axis=-1, keepdims=True)
    spread = jnp.mean(center * center, axis=-1, keepdims=True)
    rstd = lax.rsqrt(spread + EPS)
    return center * rstd, rstd


def layer_norm_back(grad, xhat, rstd):
    first = jnp.mean(grad, axis=-1, keepdims=True)
    second = jnp.mean(grad * xhat, axis=-1, keepdims=True)
    return rstd * (grad - first - xhat * second)


def total_rows(x):
    return jnp.sum(x, axis=0, keepdims=True)


def block_forward(s, x, mod, w8, f2, b1, kept):
    xa, ra, a_low, qkv, probs, o_low, att, xm, rm, m_low, gp, g_low, branch = kept
    xhat, rstd = layer_norm(x)
    xa[s] = xhat
    ra[s] = rstd
    a_low[s] = (xhat * (1.0 + mod[s, 1:2]) + mod[s, 0:1]).astype(BF16)
    for j in range(3):
        qkv[s, :, cols(j)] = dot(a_low[s], w8[s, j]).astype(BF16)
    for h in range(HEADS):
        q = qkv[s, :, cols(h, HEAD_DIM)] * 0.125
        k = qkv[s, :, cols(HEADS + h, HEAD_DIM)]
        v = qkv[s, :, cols(2 * HEADS + h, HEAD_DIM)]
        scores = dot(q, k, NT)
        e = jnp.exp(scores - jnp.max(scores, axis=-1, keepdims=True))
        p = (e * (1.0 / jnp.sum(e, axis=-1, keepdims=True))).astype(BF16)
        probs[s, h] = p
        o_low[s, :, cols(h, HEAD_DIM)] = dot(p, v).astype(BF16)
    attended = dot(o_low[s], w8[s, 3])
    att[s] = attended
    x1 = x + mod[s, 2:3] * attended
    xhat, rstd = layer_norm(x1)
    xm[s] = xhat
    rm[s] = rstd
    m_low[s] = (xhat * (1.0 + mod[s, 4:5]) + mod[s, 3:4]).astype(BF16)
    for j in range(4):
        u = dot(m_low[s], w8[s, 4 + j]) + b1[s, :, cols(j)]
        u2 = u * u
        t = jnp.tanh(GELU_A * u * (1.0 + GELU_B * u2))
        half = 0.5 * (1.0 + t)
        g_low[s, :, cols(j)] = (u * half).astype(BF16)
        gp[s, :, cols(j)] = half + (0.5 * GELU_A) * u * (1.0 - t * t) * (
            1.0 + (3.0 * GELU_B) * u2
        )
    r = dot(g_low[s], f2[s])
    branch[s] = r
    return x1 + mod[s, 5:6] * r


def block_backward(s, dy, mod, w8, f2, kept, g8, gf2, db1, dmod, dqkv, dulow):
    xa, ra, a_low, qkv, probs, o_low, att, xm, rm, m_low, gp, g_low, branch = kept
    dmod[s, 5:6] = total_rows(dy * branch[s])
    dr = (mod[s, 5:6] * dy).astype(BF16)
    for j in range(4):
        gf2[s, cols(j)] = dot(g_low[s, :, cols(j)], dr, TN).astype(BF16)
        du = (dot(dr, f2[s, cols(j)], NT) * gp[s, :, cols(j)]).astype(BF16)
        dulow[:, cols(j)] = du
        db1[s, :, cols(j)] = total_rows(du.astype(F32))
        g8[s, 4 + j] = dot(m_low[s], du, TN).astype(BF16)
    dm = dot(dulow[:, cols(0)], w8[s, 4], NT)
    for j in range(1, 4):
        dm = dm + dot(dulow[:, cols(j)], w8[s, 4 + j], NT)
    dmod[s, 3:4] = total_rows(dm)
    dmod[s, 4:5] = total_rows(dm * xm[s])
    dx1 = dy + layer_norm_back(dm * (1.0 + mod[s, 4:5]), xm[s], rm[s])
    dmod[s, 2:3] = total_rows(dx1 * att[s])
    datt = (mod[s, 2:3] * dx1).astype(BF16)
    g8[s, 3] = dot(o_low[s], datt, TN).astype(BF16)
    do_low = dot(datt, w8[s, 3], NT).astype(BF16)
    for h in range(HEADS):
        q = qkv[s, :, cols(h, HEAD_DIM)]
        k = qkv[s, :, cols(HEADS + h, HEAD_DIM)]
        v = qkv[s, :, cols(2 * HEADS + h, HEAD_DIM)]
        do = do_low[:, cols(h, HEAD_DIM)]
        p = probs[s, h]
        dqkv[:, cols(2 * HEADS + h, HEAD_DIM)] = dot(p, do, TN).astype(BF16)
        rowsum = jnp.sum(
            do.astype(F32) * o_low[s, :, cols(h, HEAD_DIM)].astype(F32), axis=-1, keepdims=True
        )
        ds = (p.astype(F32) * (dot(do, v, NT) - rowsum)).astype(BF16)
        dqkv[:, cols(h, HEAD_DIM)] = (dot(ds, k) * 0.125).astype(BF16)
        dqkv[:, cols(HEADS + h, HEAD_DIM)] = (dot(ds, q, TN) * 0.125).astype(BF16)
    da = None
    for j in range(3):
        part = dqkv[:, cols(j)]
        g8[s, j] = dot(a_low[s], part, TN).astype(BF16)
        term = dot(part, w8[s, j], NT)
        da = term if da is None else da + term
    dmod[s, 0:1] = total_rows(da)
    dmod[s, 1:2] = total_rows(da * xa[s])
    return dx1 + layer_norm_back(da * (1.0 + mod[s, 1:2]), xa[s], ra[s])


def relay_kernel(
    x_ref, tan_ref, live_ref, mod, b1, w8, f2,
    h_ref, z_ref, dlat_ref, dh_ref, dmod, db1, g8, gf2,
    *scratch,
):
    kept = scratch[:13]
    dqkv, dulow = scratch[13:]
    live = live_ref[...]
    h = block_forward(0, x_ref[...].astype(F32), mod, w8, f2, b1, kept).astype(BF16)
    h_ref[...] = (h.astype(F32) * live).astype(BF16)
    z = block_forward(1, h.astype(F32), mod, w8, f2, b1, kept)
    z_ref[...] = (z * live).astype(BF16)
    dy = tan_ref[...].astype(F32) * live
    dh = block_backward(1, dy, mod, w8, f2, kept, g8, gf2, db1, dmod, dqkv, dulow).astype(BF16)
    dh_ref[...] = dh
    dlat_ref[...] = block_backward(
        0, dh.astype(F32), mod, w8, f2, kept, g8, gf2, db1, dmod, dqkv, dulow
    )


def relay(x, tangent, live, mod, b1, w8, f2):
    shapes = (
        ((TOK, D), BF16),
        ((TOK, D), BF16),
        ((TOK, D), F32),
        ((TOK, D), BF16),
        ((2, 6, D), F32),
        ((2, 1, FF), F32),
        ((2, 8, D, D), BF16),
        ((2, FF, D), BF16),
    )
    keeps = (
        ((2, TOK, D), F32),
        ((2, TOK, 1), F32),
        ((2, TOK, D), BF16),
        ((2, TOK, 3 * D), BF16),
        ((2, HEADS, TOK, TOK), BF16),
        ((2, TOK, D), BF16),
        ((2, TOK, D), F32),
        ((2, TOK, D), F32),
        ((2, TOK, 1), F32),
        ((2, TOK, D), BF16),
        ((2, TOK, FF), F32),
        ((2, TOK, FF), BF16),
        ((2, TOK, D), F32),
        ((TOK, 3 * D), BF16),
        ((TOK, FF), BF16),
    )
    vmem = pl.BlockSpec(memory_space=pltpu.VMEM)
    return pl.pallas_call(
        relay_kernel,
        out_shape=[jax.ShapeDtypeStruct(*s) for s in shapes],
        in_specs=[vmem] * 7,
        out_specs=[vmem] * 8,
        scratch_shapes=[pltpu.VMEM(*s) for s in keeps],
        compiler_params=pltpu.CompilerParams(vmem_limit_bytes=56 * 2**20),
        name="relay",
    )(x, tangent, live, mod, b1, w8, f2)


def chunked(w):
    return jnp.swapaxes(w.reshape(2, D, -1, D), 1, 2)


def gather_weights(wqkv, wproj, wfc1, wfc2):
    def full(w):
        g = lax.all_gather(w, ("section", "group"), axis=0, tiled=True)
        return g.reshape(2, -1, w.shape[-1])

    w8 = jnp.concatenate([chunked(full(w)) for w in (wqkv, wproj, wfc1)], axis=1)
    return w8, full(wfc2)


def reduce_weights(g8, gf2):
    groups = lax.axis_size("group")

    def owned(g):
        g = g.reshape(2 * groups, -1, g.shape[-1])
        g = lax.psum_scatter(g, ("section", "group"), scatter_dimension=0, tiled=True)
        return lax.psum(g, "rep").astype(F32)

    def part(j, n):
        return owned(jnp.swapaxes(g8[:, j : j + n], 1, 2).reshape(2, D, n * D))

    return part(0, 3), part(3, 1), part(4, 4), owned(gf2)


def swap(value):
    return lax.ppermute(value, "section", [(0, 1), (1, 0)])


def body(
    latents, cond, cotangent, live_count,
    wada, bada, wqkv, wproj, wfc1, bfc1, wfc2,
):
    core = lax.axis_index("section")
    zi = lax.axis_index("group")
    ri = lax.axis_index("rep")
    groups = lax.axis_size("group")
    reps = lax.axis_size("rep")
    rows = D // groups
    is_first = core == 0

    def pick(a):
        return lax.dynamic_index_in_dim(a, core, 0, keepdims=False)

    live = (live_count[0] > 0).astype(F32)
    x = pick(latents)
    tangent = pick(cotangent)
    conds = lax.all_gather(cond, ("group", "rep"), axis=0, tiled=True)
    silu_all = jax.nn.silu(conds).astype(BF16)
    silu_rows = lax.dynamic_slice_in_dim(silu_all, zi * rows, rows, 1)
    biases = lax.all_gather(
        jnp.concatenate([bada, bfc1], axis=1), ("section", "group"), axis=0, tiled=True
    ).reshape(2, groups, -1)
    bias_ada = biases[..., : bada.shape[1]].reshape(2, 6 * D).astype(F32)
    b1 = biases[..., bada.shape[1] :].reshape(2, 1, FF).astype(F32)
    ours = lax.dynamic_index_in_dim(
        silu_rows.reshape(groups, reps, 2, rows), ri, 1, keepdims=False
    ).reshape(groups * 2, rows)
    partial_mod = jnp.dot(ours, wada[0], preferred_element_type=F32)
    own = lax.psum_scatter(partial_mod, "group", scatter_dimension=0, tiled=True)
    mods = lax.all_gather(own, "section", axis=0, tiled=False)
    mod = (lax.dynamic_index_in_dim(mods, core, 1, keepdims=False) + bias_ada).reshape(2, 6, D)

    w8, f2 = gather_weights(wqkv, wproj, wfc1, wfc2)
    h, z, dlat, dh, dmod, db1, g8, gf2 = relay(
        x, tangent, jnp.broadcast_to(pick(live), (1, 1)), mod, b1, w8, f2
    )

    dmod_low = dmod.reshape(2, 6 * D).astype(BF16)
    small = jnp.concatenate([dmod_low, db1.reshape(2, FF).astype(BF16)], axis=1)
    everyone = lax.all_gather(small, ("group", "rep", "section"), axis=0, tiled=False)
    mine = lax.dynamic_index_in_dim(everyone, core, 1, keepdims=False)
    dmod_all = mine[:, : 6 * D]
    grad_ada = lax.dot_general(silu_rows, dmod_all, TN, preferred_element_type=F32)
    sums = jnp.sum(mine.astype(F32), axis=0)
    wide = 6 * D // groups
    grad_bada = lax.dynamic_slice_in_dim(sums[: 6 * D], zi * wide, wide, 0)
    high = FF // groups
    grad_bfc1 = lax.dynamic_slice_in_dim(sums[6 * D :], zi * high, high, 0)
    ours = lax.dynamic_index_in_dim(
        dmod_all.reshape(groups, reps, 2, 6 * D), ri, 1, keepdims=False
    ).reshape(groups * 2, 6 * D)
    dsc_part = lax.dot_general(ours, wada[0], NT, preferred_element_type=F32)
    dsc_all = lax.all_gather(dsc_part, ("section", "group"), axis=0, tiled=False)
    dsc_all = lax.dynamic_slice_in_dim(dsc_all, 2 * zi, 2, 1)
    dsc = jnp.swapaxes(dsc_all.reshape(2, groups, 2, rows), 1, 2).reshape(2, 2, D)
    sig = jax.nn.sigmoid(cond)
    dc = dsc * (sig * (1.0 + cond * (1.0 - sig)))
    low = dc[1].astype(BF16).astype(F32)
    cond_grads = jnp.where(is_first, dc[0] + low, low)

    wq, wp, w1, w2 = reduce_weights(g8, gf2)

    sent = swap((jnp.where(is_first, z, h), jnp.where(is_first, dh, dlat.astype(BF16))))
    keep = jnp.where(is_first, h, z)
    section_outputs = jnp.where(
        is_first, jnp.stack([keep, sent[0]]), jnp.stack([sent[0], keep])
    )
    kept_grad = jnp.where(is_first, dlat, dh.astype(F32))
    got = sent[1].astype(F32)
    input_grads = jnp.where(is_first, jnp.stack([kept_grad, got]), jnp.stack([got, kept_grad]))
    return (
        section_outputs[None],
        input_grads[None],
        cond_grads[None],
        grad_ada[None],
        grad_bada[None],
        wq,
        wp,
        w1,
        grad_bfc1[None],
        w2,
    )


def solution(mesh):
    data = P(("group", "rep"))
    weight = P("section", "group")
    return jax.shard_map(
        body,
        mesh=mesh,
        in_specs=(data,) * 4 + (weight,) * 7,
        out_specs=(P("section", ("group", "rep")),) * 3 + (weight,) * 7,
        check_vma=False,
    )
```

time: 584 us -> 432 us (0.74); the launches traced: 574 us -> 432 us
  waiting for transfers between devices: 284 us -> 173 us
  blocking collectives: 97.2 us -> 167 us
  matrix products: 60.4 us -> 2.22 us
  other arithmetic: 51.3 us -> 13.5 us
  Pallas kernels: 0 us -> 26.3 us
  local copies, waits for them, and re-layouts: 52.3 us -> 32.3 us
  starting transfers between devices: 8.67 us -> 1.56 us
    all_gather x3 -> x6, blocking collectives: 59.2 us -> 167 us  [the longest x1 43 us: body(): conds = lax.all_gather(cond, ('group', 'rep'), axis=0, tiled=True)]
    ppermute x6 -> x2, waiting for transfers between devices: 95.2 us -> 0.01 us  [swap(): return lax.ppermute(value, 'section', [(0, 1), (1, 0)])]
    dot_general x41 -> x3, matrix products: 60.4 us -> 2.22 us  [the longest x1 1.22 us: body(): lax.dot_general(silu_rows, dmod_all, TN, preferred_element_type=F32)]
    pallas_call x0 -> x1, Pallas kernels: none -> 26.3 us  [relay(): pl.pallas_call(relay_kernel, out_shape=[jax.ShapeDtypeStruct(*s) for s in...]
    all_gather x3, waiting for transfers between devices: 41.7 us -> 19.3 us  [full(): g = lax.all_gather(w, ('section', 'group'), axis=0, tiled=True)]
    psum x1, waiting for transfers between devices: 26.3 us -> 44.9 us  [owned(): return lax.psum(g, 'rep').astype(F32)]
    unnamed x1 -> x0, blocking collectives: 17 us -> none
    reduce_sum x21 -> x1, other arithmetic: 14.2 us -> 0.07 us  [body(): sums = jnp.sum(mine.astype(F32), axis=0)]
  transfers between devices with their start and end apart: 15 -> 11, of which waited for: 9 -> 4; matrix products, arithmetic and copies ran while one was open for 7% -> 9% of each run, Pallas kernels for 0% -> 0%
where the time goes in v1:
time: 432 us
  waiting for transfers between devices  173 us (40%)
  blocking collectives  167 us (39%)
  local copies, waits for them, and re-layouts  32.3 us (7%)
  Pallas kernels  26.3 us (6%)
  between operations  16.6 us (4%)
  other arithmetic  13.5 us (3%)
    reduce_scatter x4, waiting for transfers between devices, owned(): lax.psum_scatter(g, ('section', 'group'), scatter_dimension=0, tiled=True)  106 us
    psum x1, waiting for transfers between devices, owned(): return lax.psum(g, 'rep').astype(F32)  44.9 us
    all_gather x1, blocking collectives, body(): conds = lax.all_gather(cond, ('group', 'rep'), axis=0, tiled=True)  43 us
    all_gather x1, blocking collectives, body(): lax.all_gather(small, ('group', 'rep', 'section'), axis=0, tiled=False)  42.5 us
    all_gather x1, blocking collectives, full(): g = lax.all_gather(w, ('section', 'group'), axis=0, tiled=True)  30.2 us
    pallas_call x1, Pallas kernels, relay(): pl.pallas_call(relay_kernel, out_shape=[jax.ShapeDtypeStruct(*s) for s in...  26.3 us
    all_gather x1, blocking collectives, body(): lax.all_gather(dsc_part, ('section', 'group'), axis=0, tiled=False)  25.3 us
    all_gather x1, blocking collectives, body(): lax.all_gather(jnp.concatenate([bada, bfc1], axis=1), ('section', 'group'...  24 us
  transfers between devices with their start and end apart: 11, of which 4 were waited for; matrix products, arithmetic and copies ran while one was open for 9% of the time, Pallas kernels for 0%

profile of v1, /device:TPU:0, one launch (start us, length us, event | category | flops | bytes accessed | tf_op | source)
XLA Modules:
  0.0 431.7 jit_solution(3418771400713078552)
XLA Ops:
  8.1 43.0 %all-gather.3 = f32[16,2,384]{2,1,0:T(2,128)S(1)} all-gather(f32[1,2,384]{2,1,0:T(2,128)} %bitcast.73), channel_id=1, replica_groups=mesh['section'=2,'group'=4,'rep'=4] {'group','rep'}, dimensions={0}, use_global_device_ids=true | all-gather | bytes 52224 | tf_op jit(solution)/shard_map/all_gather | solution.py:241
  54.7 24.0 %all-gather.5 = bf16[8,1,960]{2,1,0:T(2,128)(2,1)S(1)} all-gather(bf16[1,1,960]{2,1,0:T(2,128)(2,1)S(1)} %maximum_bitcast_fusion.1), channel_id=1, replica_groups=mesh['section'=2,'group'=4,'rep'=4] {'section','group'}, dimensions={0}, use_global_device_ids=true | all-gather | bytes 17280 | tf_op jit(solution)/shard_map/all_gather | solution.py:244
  79.5 1.2 dynamic-slice.3
  82.7 1.8 dynamic-slice_bitcast_fusion
  84.5 30.2 %all_gather.41 = bf16[8,96,384]{2,1,0:T(8,128)(2,1)S(1)} all-gather(bf16[1,96,384]{2,1,0:T(8,128)(2,1)S(1)} %copy-done.7), channel_id=1, replica_groups=mesh['section'=2,'group'=4,'rep'=4] {'section','group'}, dimensions={0}, use_global_device_ids=true | all-gather | bytes 663552 | tf_op jit(solution)/shard_map/all_gather | solution.py:198
  114.7 0.9 dynamic-slice_bitcast_fusion.2
  115.6 1.8 all-gather.4
  118.1 3.3 reshape.230
  121.4 1.5 copy.63
  122.9 4.2 reshape_reshape.13
  127.4 1.1 copy-done.1
  128.5 2.5 pad_maximum_fusion.w8
  131.0 19.3 %all-gather.15.cloned.1.call-done = bf16[8,384,384]{2,1,0:T(8,128)(2,1)} async-done(((bf16[1,384,384]{2,1,0:T(8,128)(2,1)}), bf16[8,384,384]{2,1,0:T(8,128)(2,1)}) %all-gather.15.cloned.1.call-update) | async-done | bytes 2359312 | tf_op jit(solution)/shard_map/all_gather | solution.py:198
  150.3 26.3 %relay.1 = (bf16[256,384]{1,0:T(8,128)(2,1)}, bf16[256,384]{1,0:T(8,128)(2,1)}, f32[256,384]{1,0:T(8,128)}, bf16[256,384]{1,0:T(8,128)(2,1)}, f32[2,6,384]{2,1,0...) custom-call(bf16[256,384]{1,0:T(8,128)(2,1)} %get-tuple-element.45.x_ref, ...), custom_call_target="tpu_custom_call" | custom-call | tf_op jit(solution)/shard_map/relay/pallas_call | solution.py:181
  176.6 1.9 slice.38
  178.6 1.7 slice_bitcast_fusion.1
  180.3 1.5 copy.49
  181.8 3.2 reshape.231
  185.1 1.9 slice_bitcast_fusion
  187.0 1.8 copy.46
  188.8 2.3 reshape_reshape.15
  192.0 42.5 %all-gather.6 = bf16[32,2,3840]{2,1,0:T(2,128)(2,1)S(1)} all-gather(bf16[1,2,3840]{2,1,0:T(2,128)(2,1)S(1)} %maximum_bitcast_fusion), channel_id=3, replica_groups=mesh['section'=2,'group'=4,'rep'=4] {'group','rep','section'}, dimensions={0}, use_global_device_ids=true | all-gather | bytes 506880 | tf_op jit(solution)/shard_map/all_gather | solution.py:264
  235.5 25.3 %all-gather.2 = f32[64,96]{1,0:T(8,128)S(1)} all-gather(f32[8,96]{1,0:T(8,128)S(1)} %fusion), channel_id=4, replica_groups=mesh['section'=2,'group'=4,'rep'=4] {'section','group'}, dimensions={0}, use_global_device_ids=true | all-gather | bytes 27648 | tf_op jit(solution)/shard_map/all_gather | solution.py:277
  261.8 50.7 %reduce-scatter.9.cloned.1.call-done = bf16[1,96,1536]{2,1,0:T(8,128)(2,1)} async-done(((bf16[8,96,1536]{2,1,0:T(8,128)(2,1)}), bf16[1,96,1536]{2,1,0:T(8,128)(2,1)}) %reduce-scatter.9.cloned.1.call-update) | async-done | bytes 294928 | tf_op jit(solution)/shard_map/reduce_scatter | solution.py:210
  312.5 55.4 %reduce-scatter.11.cloned.1.call-done = bf16[1,384,384]{2,1,0:T(8,128)(2,1)} async-done(((bf16[8,384,384]{2,1,0:T(8,128)(2,1)}), bf16[1,384,384]{2,1,0:T(8,128)(2,1)}) %reduce-scatter.11.cloned.1.call-update) | async-done | bytes 294928 | tf_op jit(solution)/shard_map/reduce_scatter | solution.py:210
  370.3 1.2 convolution_bitcast_fusion
  371.5 0.8 maximum_select_fusion.1
  372.4 0.9 maximum_select_fusion
  373.3 44.9 %all-reduce.7.cloned.1.call-done = (bf16[1,96,1152]{2,1,0:T(8,128)(2,1)}, bf16[1,96,384]{2,1,0:T(8,128)(2,1)}, bf16[1,96,1536]{2,1,0:T(8,128)(2,1)}, bf16[1,384,384]{2,1,0:T(8,128)(2,1)}) async-done(((bf16[1,96,1152]{2,1,0:T(8,128)(2,1)}, bf16[1,96,384]{2,1,0:T(8,128)(2,1)}, bf16[1,96,1536]{2,1,0:T(8,128)(2,1)}, bf16[1,384,384]{2,1,0:T(8,128)(2,1)}), (bf16[1,96,1152]{2,1,0:T(8,128)(2,1)}, ...) | async-done | bytes 884752 | tf_op jit(solution)/shard_map/psum | solution.py:211
  418.2 1.9 convert_element_type.75
  420.1 1.8 convert_element_type.76
  421.9 1.7 convert_element_type.73
  (94 shorter events, 12.5 us)
Async XLA Ops:
  8.0 43.2 %copy-start = (bf16[1,96,2304]{2,1,0:T(8,128)(2,1)S(1)}, bf16[1,96,2304]{2,1,0:T(8,128)(2,1)}, u32[]{:S(2)}) copy-start(bf16[1,96,2304]{2,1,0:T(8,128)(2,1)} %param.15) | copy-start | bytes 1327108
  8.0 76.5 %copy-start.7 = (bf16[1,96,384]{2,1,0:T(8,128)(2,1)S(1)}, bf16[1,96,384]{2,1,0:T(8,128)(2,1)}, u32[]{:S(2)}) copy-start(bf16[1,96,384]{2,1,0:T(8,128)(2,1)} %param.18) | copy-start | bytes 221188
  8.0 106.6 %all-reduce.5.cloned.1.call-start = ((), (), s32[]{:S(2)}) async-start(), calls=%async_computation.11 | async-start | bytes 147456
  52.1 66.0 %all-gather.11.cloned.1.call-start = ((), (), s32[]{:S(2)}) async-start(), calls=%async_computation.4 | async-start | bytes 1990656 | tf_op jit(solution)/shard_map/all_gather | solution.py:198
  52.7 70.2 %all-gather.13.cloned.1.call-start = ((), (), s32[]{:S(2)}) async-start(), calls=%async_computation.5 | async-start | bytes 2654208 | tf_op jit(solution)/shard_map/all_gather | solution.py:198
  53.3 97.1 %all-gather.15.cloned.1.call-start = ((), (), s32[]{:S(2)}) async-start(), calls=%async_computation.6 | async-start | bytes 2654208 | tf_op jit(solution)/shard_map/all_gather | solution.py:198
  53.8 207.9 %reduce-scatter.7.cloned.1.call-start = ((), (), s32[]{:S(2)}) async-start(), calls=%async_computation.8 | async-start | bytes 663552 | tf_op jit(solution)/shard_map/reduce_scatter | solution.py:210
  127.1 1.5 copy-start.1
  178.6 83.2 %reduce-scatter.5.cloned.1.call-start = ((), (), s32[]{:S(2)}) async-start(), calls=%async_computation.7 | async-start | bytes 1990656 | tf_op jit(solution)/shard_map/reduce_scatter | solution.py:210
  185.0 127.5 %reduce-scatter.9.cloned.1.call-start = ((), (), s32[]{:S(2)}) async-start(), calls=%async_computation.9 | async-start | bytes 2654208 | tf_op jit(solution)/shard_map/reduce_scatter | solution.py:210
  191.2 0.7 copy-start.9
  191.2 0.8 copy-start.8
  191.2 0.8 copy-start.10
  191.2 176.7 %reduce-scatter.11.cloned.1.call-start = ((), (), s32[]{:S(2)}) async-start(), calls=%async_computation.10 | async-start | bytes 2654208 | tf_op jit(solution)/shard_map/reduce_scatter | solution.py:210
  191.8 69.0 %copy-start.4 = (bf16[256,384]{1,0:T(8,128)(2,1)S(1)}, bf16[256,384]{1,0:T(8,128)(2,1)}, u32[]{:S(2)}) copy-start(bf16[256,384]{1,0:T(8,128)(2,1)} %get-tuple-element.18) | copy-start | bytes 589828
  191.8 69.0 %copy-start.5 = (bf16[256,384]{1,0:T(8,128)(2,1)S(1)}, bf16[256,384]{1,0:T(8,128)(2,1)}, u32[]{:S(2)}) copy-start(bf16[256,384]{1,0:T(8,128)(2,1)} %get-tuple-element.19) | copy-start | bytes 589828
  191.8 69.8 %copy-start.2 = (f32[256,384]{1,0:T(8,128)S(1)}, f32[256,384]{1,0:T(8,128)}, u32[]{:S(2)}) copy-start(f32[256,384]{1,0:T(8,128)} %get-tuple-element.20) | copy-start | bytes 1179652
  191.8 69.8 %copy-start.3 = (bf16[256,384]{1,0:T(8,128)(2,1)S(1)}, bf16[256,384]{1,0:T(8,128)(2,1)}, u32[]{:S(2)}) copy-start(bf16[256,384]{1,0:T(8,128)(2,1)} %get-tuple-element.21) | copy-start | bytes 589828
  191.8 226.4 %all-reduce.7.cloned.1.call-start = ((), (), s32[]{:S(2)}) async-start(), calls=%async_computation.12 | async-start | bytes 1769472 | tf_op jit(solution)/shard_map/psum | solution.py:211
  260.9 110.6 %collective-permute-start = (bf16[256,384]{1,0:T(8,128)(2,1)S(1)}, bf16[256,384]{1,0:T(8,128)(2,1)S(1)}, u32[]{:S(2)}, u32[]{:S(2)}) collective-permute-start(bf16[256,384]{1,0:T(8,128)(2,1)S(1)} %get-tuple-element.43), channel_id=1, source_target_pairs={{0,16},{16,0},{1,17},{17,1},{2,18},{18,2},{3,19},{19,3},{4,20},{20... | collective-permute-start | bytes 589832 | tf_op jit(solution)/shard_map/ppermute | solution.py:220
  369.8 2.5 collective-permute-start.1
  418.2 5.4 %copy-start.6 = (bf16[1,96,384]{2,1,0:T(8,128)(2,1)S(1)}, bf16[1,96,384]{2,1,0:T(8,128)(2,1)}, u32[]{:S(2)}) copy-start(bf16[1,96,384]{2,1,0:T(8,128)(2,1)} %get-tuple-element.37) | copy-start | bytes 221188
Sparse Core Ops, SparseCore 0:
  52.2 34.7 all-reduce.4
  368.1 50.1 all-reduce.6
Sparse Core Ops, SparseCore 1:
  54.3 23.1 all-gather.10
  79.0 40.8 all-gather.12
  121.4 28.9 all-gather.14
  178.6 31.9 reduce-scatter.6
  213.1 43.2 reduce-scatter.4
  258.8 53.6 reduce-scatter.8
  314.8 53.0 reduce-scatter.10

commit v2 on v1

--- a/solution.py
+++ b/solution.py
@@ -189,31 +189,380 @@
     )(x, tangent, live, mod, b1, w8, f2)
 
 
-def chunked(w):
-    return jnp.swapaxes(w.reshape(2, D, -1, D), 1, 2)
-
-
-def gather_weights(wqkv, wproj, wfc1, wfc2):
-    def full(w):
-        g = lax.all_gather(w, ("section", "group"), axis=0, tiled=True)
-        return g.reshape(2, -1, w.shape[-1])
-
-    w8 = jnp.concatenate([chunked(full(w)) for w in (wqkv, wproj, wfc1)], axis=1)
-    return w8, full(wfc2)
-
-
-def reduce_weights(g8, gf2):
+MESH = pl.DeviceIdType.MESH
+
+
+def places():
+    core, z, r = (lax.axis_index(n) for n in ("section", "group", "rep"))
+    return core, z, r, lax.axis_size("group"), lax.axis_size("rep")
+
+
+def remote(src, dst, sems, target):
+    return pltpu.make_async_remote_copy(
+        src_ref=src,
+        dst_ref=dst,
+        send_sem=sems[0],
+        recv_sem=sems[1],
+        device_id=target,
+        device_id_type=MESH,
+    )
+
+
+def gather_kernel(
+    cond, bias, wada, wqkv, wproj, wfc1, wfc2,
+    w8, f2, pin,
+    condbuf, pout, lsem, csem, psem, onesem, twosem, sibsem,
+):
+    core, z, r, groups, reps = places()
+    quarter = lax.rem(r, 4)
+    base = r - quarter
+    sib = 1 - core
+    local = []
+    for j in range(8):
+        if j < 3:
+            src = wqkv.at[:, cols(j)]
+        elif j == 3:
+            src = wproj
+        else:
+            src = wfc1.at[:, cols(j - 4)]
+        local.append(pltpu.make_async_copy(src, w8.at[core, j, z], lsem.at[j]))
+    local.append(pltpu.make_async_copy(wfc2, f2.at[core, z], lsem.at[8]))
+    for copy in local:
+        copy.start()
+
+    sends = []
+    for d in range(1, groups):
+        to = lax.rem(z + d, groups)
+        copy = remote(
+            cond.at[to], condbuf.at[z], (csem.at[0, d - 1], csem.at[1, d - 1]), (core, to, r)
+        )
+        copy.start()
+        sends.append(copy)
+    condbuf[z] = cond[z]
+
+    for copy in local:
+        copy.wait()
+
+    def piece(zz, qq):
+        return w8.at[core, pl.ds(2 * qq, 2), zz], f2.at[core, zz, qq]
+
+    def shard(cc, zz):
+        return w8.at[cc, :, zz], f2.at[cc, zz]
+
+    def both(refs, sems, target):
+        return [
+            remote(ref, ref, (sems(0, i), sems(1, i)), target) for i, ref in enumerate(refs)
+        ]
+
+    def one(d, zz, target):
+        return both(piece(zz, quarter), lambda k, i: onesem.at[k, d - 1, i], target)
+
+    def two(d, e, zz, qq, target):
+        return both(piece(zz, qq), lambda k, i: twosem.at[k, d - 1, e - 1, i], target)
+
+    def three(d, cc, zz, target):
+        return both(shard(cc, zz), lambda k, i: sibsem.at[k, d, i], target)
+
+    def launch(copies):
+        for copy in copies:
+            copy.start()
+            sends.append(copy)
+
+    for d in range(1, groups):
+        to = lax.rem(z + d, groups)
+        launch(one(d, z, (core, to, r)))
+    launch(three(0, core, z, (sib, z, r)))
+
+    for d in range(1, groups):
+        came = lax.rem(z + groups - d, groups)
+        remote(
+            cond.at[came], condbuf.at[came], (csem.at[0, d - 1], csem.at[1, d - 1]), (core, came, r)
+        ).wait_recv()
+    for zz in range(groups):
+        c = condbuf[zz]
+        silu = (c / (1.0 + jnp.exp(-c))).astype(BF16)
+        pout[zz, 0:2] = dot(silu, wada[...])
+        pout[zz, 2:3] = bias[...]
+    pin[core, z] = pout[z]
+
+    hops = [(d, k) for d in range(groups) for k in range(2) if (d, k) != (0, 0)]
+    for d, k in hops:
+        to = lax.rem(z + d, groups)
+        copy = remote(
+            pout.at[to],
+            pin.at[core, z],
+            (psem.at[0, d, k], psem.at[1, d, k]),
+            (sib if k else core, to, r),
+        )
+        copy.start()
+        sends.append(copy)
+
+    for d in range(1, groups):
+        came = lax.rem(z + groups - d, groups)
+        for copy in one(d, came, (core, came, r)):
+            copy.wait_recv()
+        for e in range(1, 4):
+            launch(two(d, e, came, quarter, (core, z, base + lax.rem(quarter + e, 4))))
+    for d in range(1, groups):
+        came = lax.rem(z + groups - d, groups)
+        for e in range(1, 4):
+            theirs = lax.rem(quarter + 4 - e, 4)
+            for copy in two(d, e, came, theirs, (core, z, base + theirs)):
+                copy.wait_recv()
+        launch(three(d, core, came, (sib, z, r)))
+    for d, k in hops:
+        came = lax.rem(z + groups - d, groups)
+        remote(
+            pout.at[came],
+            pin.at[sib if k else core, came],
+            (psem.at[0, d, k], psem.at[1, d, k]),
+            (sib if k else core, came, r),
+        ).wait_recv()
+    for d in range(groups):
+        came = lax.rem(z + groups - d, groups)
+        for copy in three(d, sib, came, (sib, z, r)):
+            copy.wait_recv()
+    for copy in sends:
+        copy.wait_send()
+
+
+def gather_all(cond, bias, wada, wqkv, wproj, wfc1, wfc2):
     groups = lax.axis_size("group")
-
-    def owned(g):
-        g = g.reshape(2 * groups, -1, g.shape[-1])
-        g = lax.psum_scatter(g, ("section", "group"), scatter_dimension=0, tiled=True)
-        return lax.psum(g, "rep").astype(F32)
-
-    def part(j, n):
-        return owned(jnp.swapaxes(g8[:, j : j + n], 1, 2).reshape(2, D, n * D))
-
-    return part(0, 3), part(3, 1), part(4, 4), owned(gf2)
+    rows = D // groups
+    vmem = pl.BlockSpec(memory_space=pltpu.VMEM)
+    hbm = pl.BlockSpec(memory_space=pl.ANY)
+    dma = pltpu.SemaphoreType.DMA
+    return pl.pallas_call(
+        gather_kernel,
+        out_shape=[
+            jax.ShapeDtypeStruct((2, 8, groups, rows, D), BF16),
+            jax.ShapeDtypeStruct((2, groups, 4, rows, D), BF16),
+            jax.ShapeDtypeStruct((2, groups, 3, 6 * D), F32),
+        ],
+        in_specs=[vmem] * 3 + [hbm] * 4,
+        out_specs=[vmem] * 3,
+        scratch_shapes=[
+            pltpu.VMEM((groups, 2, rows), F32),
+            pltpu.VMEM((groups, 3, 6 * D), F32),
+            dma((9,)),
+            dma((2, groups - 1)),
+            dma((2, groups, 2)),
+            dma((2, groups - 1, 2)),
+            dma((2, groups - 1, 3, 2)),
+            dma((2, groups, 2)),
+        ],
+        compiler_params=pltpu.CompilerParams(vmem_limit_bytes=40 * 2**20, has_side_effects=True),
+        name="gather_all",
+    )(cond, bias, wada, wqkv, wproj, wfc1, wfc2)
+
+
+def reduce_kernel(
+    small, wada, g8, gf2,
+    fin, every, dsc,
+    ra8, raf, sb8, sbf, rb8, rbf, tc, rc, dout,
+    allsend, allrecv, asem, bsem, zsem, fsem, dsem,
+):
+    core, z, r, groups, reps = places()
+    quarter = lax.rem(r, 4)
+    base = r - quarter
+    sib = 1 - core
+    total = 2 * groups * reps
+    me = (z * reps + r) * 2 + core
+    sends = []
+
+    def launch(copies):
+        for copy in copies:
+            copy.start()
+            sends.append(copy)
+
+    def sibling(e, qq):
+        return [
+            remote(
+                g8.at[sib, pl.ds(2 * qq, 2)],
+                ra8.at[e],
+                (asem.at[0, e, 0], asem.at[1, e, 0]),
+                (sib, z, r),
+            ),
+            remote(
+                gf2.at[sib, :, qq], raf.at[e], (asem.at[0, e, 1], asem.at[1, e, 1]), (sib, z, r)
+            ),
+        ]
+
+    order = (1, 2, 3, 0)
+    for e in order:
+        launch(sibling(e, lax.rem(quarter + e, 4)))
+
+    def spread(i):
+        other = lax.rem(me + i, total)
+        there = lax.rem(other, 2)
+        chip = other // 2
+        return remote(
+            small.at[there],
+            every.at[me],
+            (allsend.at[i], allrecv.at[i]),
+            (there, chip // reps, lax.rem(chip, reps)),
+        )
+
+    def collect(i):
+        other = lax.rem(me + total - i, total)
+        chip = other // 2
+        return remote(
+            small.at[core],
+            every.at[other],
+            (allsend.at[i], allrecv.at[i]),
+            (lax.rem(other, 2), chip // reps, lax.rem(chip, reps)),
+        )
+
+    def start_one(i, carry):
+        spread(i).start()
+        return carry
+
+    lax.fori_loop(1, total, start_one, 0)
+    every[me] = small[core]
+
+    def across(e, to):
+        return [
+            remote(
+                sb8.at[e], rb8.at[e - 1], (bsem.at[0, e - 1, 0], bsem.at[1, e - 1, 0]), (core, z, to)
+            ),
+            remote(
+                sbf.at[e], rbf.at[e - 1], (bsem.at[0, e - 1, 1], bsem.at[1, e - 1, 1]), (core, z, to)
+            ),
+        ]
+
+    for e in order:
+        qq = lax.rem(quarter + e, 4)
+        for copy in sibling(e, qq):
+            copy.wait_recv()
+        for i in range(2):
+            sb8[e, i] = (g8[core, 2 * qq + i].astype(F32) + ra8[e, i].astype(F32)).astype(BF16)
+        sbf[e] = (gf2[core, :, qq].astype(F32) + raf[e].astype(F32)).astype(BF16)
+        if e:
+            launch(across(e, base + qq))
+
+    def collect_one(i, carry):
+        collect(i).wait_recv()
+        return carry
+
+    lax.fori_loop(1, total, collect_one, 0)
+    for zz in range(groups):
+        at = (zz * reps + r) * 2
+        rows2 = jnp.concatenate(
+            [every[at, :, : 6 * D], every[at + 1, :, : 6 * D]], axis=0
+        ).astype(BF16)
+        dout[zz] = dot(rows2, wada[...], NT)
+    dsc[core, z] = dout[z]
+    hops = [(d, k) for d in range(groups) for k in range(2) if (d, k) != (0, 0)]
+    for d, k in hops:
+        to = lax.rem(z + d, groups)
+        launch(
+            [
+                remote(
+                    dout.at[to],
+                    dsc.at[core, z],
+                    (dsem.at[0, d, k], dsem.at[1, d, k]),
+                    (sib if k else core, to, r),
+                )
+            ]
+        )
+
+    for e in range(1, 4):
+        theirs = base + lax.rem(quarter + 4 - e, 4)
+        for copy in across(e, theirs):
+            copy.wait_recv()
+    for zz in range(groups):
+        for i in range(2):
+            t = sb8[0, i, zz].astype(F32)
+            for e in range(3):
+                t = t + rb8[e, i, zz].astype(F32)
+            tc[zz, i] = t.astype(BF16)
+        t = sbf[0, zz].astype(F32)
+        for e in range(3):
+            t = t + rbf[e, zz].astype(F32)
+        tc[zz, 2] = t.astype(BF16)
+
+    def along(d, zz, target):
+        return remote(tc.at[zz], rc.at[d - 1], (zsem.at[0, d - 1], zsem.at[1, d - 1]), target)
+
+    for d in range(1, groups):
+        to = lax.rem(z + d, groups)
+        launch([along(d, to, (core, to, r))])
+    for d in range(1, groups):
+        came = lax.rem(z + groups - d, groups)
+        along(d, came, (core, came, r)).wait_recv()
+    for i in range(3):
+        t = tc[z, i].astype(F32)
+        for d in range(groups - 1):
+            t = t + rc[d, i].astype(F32)
+        fin[quarter, i] = t.astype(BF16)
+
+    def share(e, qq, to):
+        return remote(fin.at[qq], fin.at[qq], (fsem.at[0, e - 1], fsem.at[1, e - 1]), (core, z, to))
+
+    for e in range(1, 4):
+        launch([share(e, quarter, base + lax.rem(quarter + e, 4))])
+    for e in range(1, 4):
+        theirs = lax.rem(quarter + 4 - e, 4)
+        share(e, theirs, base + theirs).wait_recv()
+    for d, k in hops:
+        came = lax.rem(z + groups - d, groups)
+        who = sib if k else core
+        remote(
+            dout.at[came],
+            dsc.at[who, came],
+            (dsem.at[0, d, k], dsem.at[1, d, k]),
+            (who, came, r),
+        ).wait_recv()
+
+    def finish_one(i, carry):
+        spread(i).wait_send()
+        return carry
+
+    lax.fori_loop(1, total, finish_one, 0)
+    for copy in sends:
+        copy.wait_send()
+
+
+def reduce_all(small, wada, g8, gf2):
+    groups, reps = lax.axis_size("group"), lax.axis_size("rep")
+    rows = D // groups
+    total = 2 * groups * reps
+    width = small.shape[-1]
+    vmem = pl.BlockSpec(memory_space=pltpu.VMEM)
+    dma = pltpu.SemaphoreType.DMA
+    fin, every, dsc = pl.pallas_call(
+        reduce_kernel,
+        out_shape=[
+            jax.ShapeDtypeStruct((4, 3, rows, D), BF16),
+            jax.ShapeDtypeStruct((total, 1, width), F32),
+            jax.ShapeDtypeStruct((2, groups, 2, rows), F32),
+        ],
+        in_specs=[vmem] * 4,
+        out_specs=[vmem] * 3,
+        scratch_shapes=[
+            pltpu.VMEM((4, 2, groups, rows, D), BF16),
+            pltpu.VMEM((4, groups, rows, D), BF16),
+            pltpu.VMEM((4, 2, groups, rows, D), BF16),
+            pltpu.VMEM((4, groups, rows, D), BF16),
+            pltpu.VMEM((3, 2, groups, rows, D), BF16),
+            pltpu.VMEM((3, groups, rows, D), BF16),
+            pltpu.VMEM((groups, 3, rows, D), BF16),
+            pltpu.VMEM((groups - 1, 3, rows, D), BF16),
+            pltpu.VMEM((groups, 2, rows), F32),
+            dma((total,)),
+            dma((total,)),
+            dma((2, 4, 2)),
+            dma((2, 3, 2)),
+            dma((2, groups - 1)),
+            dma((2, 3)),
+            dma((2, groups, 2)),
+        ],
+        compiler_params=pltpu.CompilerParams(vmem_limit_bytes=48 * 2**20, has_side_effects=True),
+        name="reduce_all",
+    )(small, wada, g8.reshape(2, 8, groups, rows, D), gf2.reshape(2, groups, 4, rows, D))
+    if reps > 4:
+        fin = (lax.psum(fin, "rep").astype(F32) * 0.25).astype(BF16)
+    return fin.astype(F32), every, dsc
 
 
 def swap(value):
@@ -226,9 +575,7 @@
 ):
     core = lax.axis_index("section")
     zi = lax.axis_index("group")
-    ri = lax.axis_index("rep")
     groups = lax.axis_size("group")
-    reps = lax.axis_size("rep")
     rows = D // groups
     is_first = core == 0
 
@@ -238,51 +585,52 @@
     live = (live_count[0] > 0).astype(F32)
     x = pick(latents)
     tangent = pick(cotangent)
-    conds = lax.all_gather(cond, ("group", "rep"), axis=0, tiled=True)
-    silu_all = jax.nn.silu(conds).astype(BF16)
-    silu_rows = lax.dynamic_slice_in_dim(silu_all, zi * rows, rows, 1)
-    biases = lax.all_gather(
-        jnp.concatenate([bada, bfc1], axis=1), ("section", "group"), axis=0, tiled=True
-    ).reshape(2, groups, -1)
-    bias_ada = biases[..., : bada.shape[1]].reshape(2, 6 * D).astype(F32)
-    b1 = biases[..., bada.shape[1] :].reshape(2, 1, FF).astype(F32)
-    ours = lax.dynamic_index_in_dim(
-        silu_rows.reshape(groups, reps, 2, rows), ri, 1, keepdims=False
-    ).reshape(groups * 2, rows)
-    partial_mod = jnp.dot(ours, wada[0], preferred_element_type=F32)
-    own = lax.psum_scatter(partial_mod, "group", scatter_dimension=0, tiled=True)
-    mods = lax.all_gather(own, "section", axis=0, tiled=False)
-    mod = (lax.dynamic_index_in_dim(mods, core, 1, keepdims=False) + bias_ada).reshape(2, 6, D)
-
-    w8, f2 = gather_weights(wqkv, wproj, wfc1, wfc2)
+    cond_cols = jnp.swapaxes(cond.reshape(2, groups, rows), 0, 1)
+    bias = jnp.concatenate([bada, bfc1], axis=1).astype(F32)
+    bias = jnp.pad(bias, ((0, 0), (0, 6 * D - bias.shape[1])))
+    w8, f2, pin = gather_all(
+        cond_cols, bias, wada[0], wqkv[0], wproj[0], wfc1[0], wfc2[0].reshape(4, rows, D)
+    )
+    w8 = w8.reshape(2, 8, D, D)
+    f2 = f2.reshape(2, FF, D)
+    wide = 6 * D // groups
+    high = FF // groups
+    bias_ada = pin[:, :, 2, :wide].reshape(2, 6 * D)
+    b1 = pin[:, :, 2, wide : wide + high].reshape(2, 1, FF)
+    sums = jnp.sum(pin[:, :, :2], axis=1)
+    mod = (lax.dynamic_index_in_dim(sums, core, 1, keepdims=False) + bias_ada).reshape(2, 6, D)
+
     h, z, dlat, dh, dmod, db1, g8, gf2 = relay(
         x, tangent, jnp.broadcast_to(pick(live), (1, 1)), mod, b1, w8, f2
     )
 
-    dmod_low = dmod.reshape(2, 6 * D).astype(BF16)
-    small = jnp.concatenate([dmod_low, db1.reshape(2, FF).astype(BF16)], axis=1)
-    everyone = lax.all_gather(small, ("group", "rep", "section"), axis=0, tiled=False)
-    mine = lax.dynamic_index_in_dim(everyone, core, 1, keepdims=False)
-    dmod_all = mine[:, : 6 * D]
+    def rounded(v):
+        return v.astype(BF16).astype(F32)
+
+    dmod_low = rounded(dmod.reshape(2, 1, 6 * D))
+    silu = jnp.broadcast_to(rounded(jax.nn.silu(pick(cond))), (2, 1, D))
+    small = jnp.concatenate([dmod_low, db1, silu], axis=-1)
+    fin, every, dsc_all = reduce_all(small, wada[0], g8, gf2)
+    every = every[:, 0]
+    dmod_all = every[:, : 6 * D].astype(BF16)
+    silu_rows = lax.dynamic_slice_in_dim(every[:, 6 * D + FF :], zi * rows, rows, 1).astype(BF16)
     grad_ada = lax.dot_general(silu_rows, dmod_all, TN, preferred_element_type=F32)
-    sums = jnp.sum(mine.astype(F32), axis=0)
-    wide = 6 * D // groups
+    sums = jnp.sum(every[:, : 6 * D + FF], axis=0)
     grad_bada = lax.dynamic_slice_in_dim(sums[: 6 * D], zi * wide, wide, 0)
-    high = FF // groups
     grad_bfc1 = lax.dynamic_slice_in_dim(sums[6 * D :], zi * high, high, 0)
-    ours = lax.dynamic_index_in_dim(
-        dmod_all.reshape(groups, reps, 2, 6 * D), ri, 1, keepdims=False
-    ).reshape(groups * 2, 6 * D)
-    dsc_part = lax.dot_general(ours, wada[0], NT, preferred_element_type=F32)
-    dsc_all = lax.all_gather(dsc_part, ("section", "group"), axis=0, tiled=False)
-    dsc_all = lax.dynamic_slice_in_dim(dsc_all, 2 * zi, 2, 1)
-    dsc = jnp.swapaxes(dsc_all.reshape(2, groups, 2, rows), 1, 2).reshape(2, 2, D)
+    dsc = jnp.swapaxes(dsc_all, 1, 2).reshape(2, 2, D)
     sig = jax.nn.sigmoid(cond)
     dc = dsc * (sig * (1.0 + cond * (1.0 - sig)))
     low = dc[1].astype(BF16).astype(F32)
     cond_grads = jnp.where(is_first, dc[0] + low, low)
 
-    wq, wp, w1, w2 = reduce_weights(g8, gf2)
+    chunks = fin[:, :2].reshape(8, rows, D)
+
+    def joined(j, n):
+        return jnp.swapaxes(chunks[j : j + n], 0, 1).reshape(1, rows, n * D)
+
+    wq, wp, w1 = joined(0, 3), joined(3, 1), joined(4, 4)
+    w2 = fin[:, 2].reshape(1, 4 * rows, D)
 
     sent = swap((jnp.where(is_first, z, h), jnp.where(is_first, dh, dlat.astype(BF16))))
     keep = jnp.where(is_first, h, z)

time: 432 us -> 202 us (0.47)
  waiting for transfers between devices: 173 us -> 0.01 us
  blocking collectives: 167 us -> 0 us
  Pallas kernels: 26.3 us -> 166 us
  between operations: 16.6 us -> 0.85 us
  local copies, waits for them, and re-layouts: 32.3 us -> 21.1 us
  other arithmetic: 13.5 us -> 8.82 us
    all_gather x6 -> x0, blocking collectives: 167 us -> none  [the longest x1 43 us: body(): conds = lax.all_gather(cond, ('group', 'rep'), axis=0, tiled=True)]
    pallas_call x0 -> x2, Pallas kernels: none -> 140 us  [the longest x1 89.3 us: reduce_all(): pl.pallas_call(reduce_kernel, out_shape=[jax.ShapeDtypeStruct((4, 3, rows...]
    reduce_scatter x4 -> x0, waiting for transfers between devices: 106 us -> none  [owned(): lax.psum_scatter(g, ('section', 'group'), scatter_dimension=0, tiled=True)]
    psum x1 -> x0, waiting for transfers between devices: 44.9 us -> none  [owned(): return lax.psum(g, 'rep').astype(F32)]
    all_gather x3 -> x0, waiting for transfers between devices: 19.3 us -> none  [full(): g = lax.all_gather(w, ('section', 'group'), axis=0, tiled=True)]
    another operation x7 -> x1, local copies, waits for them, and re-layouts: 16.3 us -> 0.09 us  [body(): bias_ada = pin[:, :, 2, :wide].reshape(2, 6 * D)]
    unnamed x28 -> x29, local copies, waits for them, and re-layouts: 3.39 us -> 10.6 us
    convert_element_type x8 -> x2, other arithmetic: 6.26 us -> 0.75 us  [rounded(): return v.astype(BF16).astype(F32)]
  transfers between devices with their start and end apart: 11 -> 2, of which waited for: 4 -> 0; matrix products, arithmetic and copies ran while one was open for 9% -> 7% of each run, Pallas kernels for 0% -> 45%
where the time goes in v2:
time: 202 us; the launch traced here: 199 us
  Pallas kernels  166 us (82%)
  local copies, waits for them, and re-layouts  21.1 us (10%)
  other arithmetic  8.82 us (4%)
    pallas_call x1, Pallas kernels, reduce_all(): pl.pallas_call(reduce_kernel, out_shape=[jax.ShapeDtypeStruct((4, 3, rows...  89.3 us
    pallas_call x1, Pallas kernels, gather_all(): pl.pallas_call(gather_kernel, out_shape=[jax.ShapeDtypeStruct((2, 8, grou...  50.3 us
    pallas_call x1, Pallas kernels, relay(): pl.pallas_call(relay_kernel, out_shape=[jax.ShapeDtypeStruct(*s) for s in...  26.3 us
    unnamed x29, local copies, waits for them, and re-layouts  10.6 us
  transfers between devices with their start and end apart: 2, of which 0 were waited for; matrix products, arithmetic and copies ran while one was open for 7% of the time, Pallas kernels for 45%

profile of v2, /device:TPU:0, one launch (start us, length us, event | category | flops | bytes accessed | tf_op | source)
XLA Modules:
  0.0 199.3 jit_solution(5451043327731644232)
XLA Ops:
  0.6 0.8 reshape.225
  1.4 0.8 fusion.1.bias
  2.2 1.0 copy-done.3
  3.2 1.0 copy-done.5
  4.2 1.0 copy-done.6
  5.1 0.9 copy-done.7
  6.1 0.9 copy-done.8
  7.0 50.3 %gather_all.1 = (bf16[2,8,4,96,384]{4,3,2,1,0:T(8,128)(2,1)S(1)}, bf16[2,4,4,96,384]{4,3,2,1,0:T(8,128)(2,1)S(1)}, f32[2,4,3,2304]{3,2,1,0:T(4,128)S(1)}) custom-call(f32[4,2,96]{2,1,0:T(2,128)S(1)} %bitcast.47, f32[1,2304]{1,0:T(1,128)S(1)} %fusion.1.bias, bf16[96,2304]{1,0:T(8,128)(2,1)S(1)} %bitcast.41, bf16[96,1152]{1,0:T(8,128)(2,1)S(1)} %bitcast.45, ...), custom_call_target="tpu_custom_call" | custom-call | tf_op jit(solution)/shard_map/gather_all/pallas_call | solution.py:335
  57.3 2.1 %copy-done = bf16[2,8,4,96,384]{4,3,2,1,0:T(8,128)(2,1)} copy-done((bf16[2,8,4,96,384]{4,3,2,1,0:T(8,128)(2,1)}, bf16[2,8,4,96,384]{4,3,2,1,0:T(8,128)(2,1)S(1)}, u32[]{:S(2)}) %copy-start) | copy-done | bytes 4718616
  59.4 1.4 copy-done.1
  60.9 0.7 slice.53
  61.8 0.7 compare_convert_fusion
  62.4 0.6 constant_dynamic-slice_fusion.live_ref
  63.0 0.6 add.41.mod
  63.6 1.8 dynamic-slice_bitcast_fusion
  65.4 26.3 %relay.1 = (bf16[256,384]{1,0:T(8,128)(2,1)}, bf16[256,384]{1,0:T(8,128)(2,1)}, f32[256,384]{1,0:T(8,128)}, bf16[256,384]{1,0:T(8,128)(2,1)}, f32[2,6,384]{2,1,0...) custom-call(bf16[256,384]{1,0:T(8,128)(2,1)} %get-tuple-element.41.x_ref, ...), custom_call_target="tpu_custom_call" | custom-call | tf_op jit(solution)/shard_map/relay/pallas_call | solution.py:181
  91.7 1.1 convert_select_fusion
  93.3 1.1 select_bitcast_fusion.1
  94.6 0.7 convert_convert_fusion
  95.4 0.7 maximum_maximum_fusion.small
  96.1 1.7 copy-done.2
  97.8 89.3 %reduce_all.1 = (bf16[4,3,96,384]{3,2,1,0:T(8,128)(2,1)S(1)}, f32[32,1,4224]{2,1,0:T(1,128)S(1)}, f32[2,4,2,96]{3,2,1,0:T(2,128)S(1)}) custom-call(f32[2,1,4224]{2,1,0:T(1,128)S(1)} %maximum_maximum_fusion.small, bf16[96,2304]{1,0:T(8,128)(2,1)S(1)} %bitcast.42, bf16[2,8,4,96,384]{4,3,2,1,0:T(8,128)(2,1)} %bitcast.49, bf16[2,4,4,96,384]{4,3,2,1,0:T(8,128)(2,1)S(1)} %bitcast.40), custom_call_target="tpu_custom_call" | custom-call | tf_op jit(solution)/shard_map/reduce_all/pallas_call | solution.py:533
  187.3 0.7 slice.75
  188.0 0.9 slice.78
  188.9 0.6 slice.69
  190.1 0.6 add_multiply_fusion
  191.1 1.0 reshape.232
  192.5 1.1 reshape.233
  195.0 2.0 %convolution_bitcast_fusion = f32[1,96,2304]{2,1,0:T(8,128)} fusion(f32[32,4224]{1,0:T(8,128)S(1)} %bitcast.52, bf16[32,384]{1,0:T(8,128)(2,1)} %slice.69, s32[]{:T(128)S(6)} %select_n.90), kind=kOutput, calls=%fused_computation | convolution fusion | flops 14155776 | bytes 1040388 | tf_op jit(solution)/shard_map/dot_general | solution.py:617
  197.0 0.6 add_select_fusion
  197.6 0.9 maximum_select_fusion
  198.5 0.8 maximum_select_fusion.1
  (53 shorter events, 4.0 us)
Async XLA Ops:
  2.2 1.0 copy-start.3
  3.2 1.0 copy-start.5
  4.2 1.0 copy-start.6
  5.1 0.9 copy-start.7
  6.1 0.9 copy-start.8
  57.3 2.1 %copy-start = (bf16[2,8,4,96,384]{4,3,2,1,0:T(8,128)(2,1)}, bf16[2,8,4,96,384]{4,3,2,1,0:T(8,128)(2,1)S(1)}, u32[]{:S(2)}) copy-start(bf16[2,8,4,96,384]{4,3,2,1,0:T(8,128)(2,1)S(1)} %get-tuple-element.25) | copy-start | bytes 14155780
  59.4 1.4 copy-start.1
  65.4 29.1 %copy-start.12 = (f32[2,384]{1,0:T(2,128)S(1)}, f32[2,384]{1,0:T(2,128)}, u32[]{:S(2)}) copy-start(f32[2,384]{1,0:T(2,128)} %param.12) | copy-start | bytes 9220
  65.4 30.7 %copy-start.4 = (bf16[1,96,2304]{2,1,0:T(8,128)(2,1)S(1)}, bf16[1,96,2304]{2,1,0:T(8,128)(2,1)}, u32[]{:S(2)}) copy-start(bf16[1,96,2304]{2,1,0:T(8,128)(2,1)} %param.15) | copy-start | bytes 1327108
  92.9 104.7 %collective-permute-start.1 = (bf16[256,384]{1,0:T(8,128)(2,1)S(1)}, bf16[256,384]{1,0:T(8,128)(2,1)S(1)}, u32[]{:S(2)}, u32[]{:S(2)}) collective-permute-start(bf16[256,384]{1,0:T(8,128)(2,1)S(1)} %convert_select_fusion), channel_id=1, source_target_pairs={{0,16},{16,0},{1,17},{17,1},{2,18},{18,2},{3,19},{19,3},{4,20},{20... | collective-permute-start | bytes 589832 | tf_op jit(solution)/shard_map/ppermute | solution.py:569
  94.3 104.2 %collective-permute-start = (bf16[256,384]{1,0:T(8,128)(2,1)S(1)}, bf16[256,384]{1,0:T(8,128)(2,1)S(1)}, u32[]{:S(2)}, u32[]{:S(2)}) collective-permute-start(bf16[256,384]{1,0:T(8,128)(2,1)S(1)} %get-tuple-element.39), channel_id=1, source_target_pairs={{0,16},{16,0},{1,17},{17,1},{2,18},{18,2},{3,19},{19,3},{4,20},{20... | collective-permute-start | bytes 589832 | tf_op jit(solution)/shard_map/ppermute | solution.py:569
  96.1 1.7 copy-start.2
  187.2 3.5 %copy-start.9 = (f32[256,384]{1,0:T(8,128)S(1)}, f32[256,384]{1,0:T(8,128)}, u32[]{:S(2)}) copy-start(f32[256,384]{1,0:T(8,128)} %get-tuple-element.29) | copy-start | bytes 1179652
  187.2 3.5 %copy-start.10 = (bf16[256,384]{1,0:T(8,128)(2,1)S(1)}, bf16[256,384]{1,0:T(8,128)(2,1)}, u32[]{:S(2)}) copy-start(bf16[256,384]{1,0:T(8,128)(2,1)} %get-tuple-element.30) | copy-start | bytes 589828
  189.6 0.6 copy-start.11
  191.1 2.5 %slice-start = ((f32[3840]{0:T(1024)}), f32[2304]{0:T(1024)S(1)}, s32[]{:S(2)}) async-start(f32[3840]{0:T(1024)} %copy-done.11), calls=%async_computation | async-start | bytes 24576 | tf_op jit(solution)/shard_map/slice | solution.py:619
  191.1 5.9 %copy-start.13 = (f32[2,384]{1,0:T(2,128)S(1)}, f32[2,384]{1,0:T(2,128)}, u32[]{:S(2)}) copy-start(f32[2,384]{1,0:T(2,128)} %add_multiply_fusion) | copy-start | bytes 9220
